TPU v7x, 32 devices: a whole 2x2x4 slice. The times are simulated.
32 devices in a mesh: aux: 2 (over core), pair: 16 (over z, y, x).
Axes of the slice: x: 2, y: 2, z: 4, core: 2. Of those that a mesh axis runs over, the one named last changes fastest.
Arguments:
- metric_factor: bfloat16 [16384, 16384], P('pair', 'aux'), as said below
- three_centre: bfloat16 [16384, 1536], P('aux', 'pair')
- occ_energy: float32 [2], replicated, may hold values from -2 to -0.3
- virt_energy: float32 [768], replicated, may hold values from 0.2 to 3
Outputs:
- amplitudes: float32 [1536, 1536], P('pair', 'aux')
- energy: float32 [], replicated
Inputs may be any that keep to these rules, and one draw needn't show every extreme that they name: metric_factor is lower triangular: every entry above the diagonal is zero, and its diagonal lies between 0.5 and 1.5.
All inputs are finite; a program needn't handle non-finite values.
Results may differ from a plain program's by a relative error of at most 0.0023.
Values may be sent and summed in bfloat16 or wider, within the bound.
No kernel may reach another device: no remote copies, remote signals or barrier semaphores. Data moves between devices by JAX's collectives and lax.ppermute only.
A program may use at most 128 MiB of HBM per device.

v0:
```python
import functools

import jax
import jax.numpy as jnp
from jax import lax
from jax.experimental import pallas as pl
from jax.experimental.pallas import tpu as pltpu
from jax.sharding import PartitionSpec as P

AXES = ("aux", "pair")
LAYERS = 4
PLANE = 4
TURN = (1, 2)


def total_of(value, axes):
    count = lax.axis_size(axes)
    sent = jnp.broadcast_to(value, (count, 8, 128))
    return jnp.sum(lax.all_to_all(sent, axes, 0, 0, tiled=True)[:, 0, 0])


def nt_dot(left, right):
    return lax.dot_general(
        left, right, (((1,), (1,)), ((), ())), preferred_element_type=jnp.float32
    )


def outputs(tiles, occ_energy, virt_energy):
    pair_count, share_rows, share_cols = tiles.shape
    aux_id = lax.axis_index("aux")
    pair_id = lax.axis_index("pair")
    integrals = jnp.sum(tiles.astype(jnp.float32), axis=0)
    pair_gap = (virt_energy[None, :] - occ_energy[:, None]).reshape(-1)
    row_gap = lax.dynamic_slice_in_dim(pair_gap, pair_id * share_rows, share_rows, 0)
    col_gap = lax.dynamic_slice_in_dim(pair_gap, aux_id * share_cols, share_cols, 0)
    denominator = row_gap[:, None] + col_gap[None, :]
    amplitudes = integrals / denominator
    energy = -total_of(jnp.sum(integrals * amplitudes), AXES)
    return (amplitudes, energy)


def shards_any(metric_factor, three_centre, occ_energy, virt_energy):
    aux_count = lax.axis_size("aux")
    pair_count = lax.axis_size("pair")
    pairs_total = three_centre.shape[1] * pair_count
    share_cols = pairs_total // aux_count
    share_rows = pairs_total // pair_count
    partial_fit = jnp.dot(
        metric_factor,
        lax.all_gather(three_centre, "pair", axis=1, tiled=True),
        preferred_element_type=jnp.float32,
    )
    own_share = lax.psum_scatter(partial_fit, "aux", scatter_dimension=1, tiled=True).astype(
        jnp.bfloat16
    )
    fitted = lax.all_gather(own_share, "aux", axis=1, tiled=True)
    partial_tiles = lax.dot_general(
        fitted, own_share, (((0,), (0,)), ((), ())), preferred_element_type=jnp.float32
    ).astype(jnp.bfloat16)
    tiles = lax.all_to_all(partial_tiles, "pair", 0, 0, tiled=True)
    return outputs(tiles.reshape(pair_count, share_rows, share_cols), occ_energy, virt_energy)


def layers_of(core):
    return range(0, LAYERS) if core == 0 else range(LAYERS // 2, LAYERS)


def along(turn):
    pairs = []
    for core in range(2):
        for z in layers_of(core):
            at = (core * LAYERS + z) * PLANE
            pairs += [(at + i, at + (i ^ turn[core])) for i in range(PLANE)]
    return pairs


def climbs(stage):
    steps = [[(z, (z + 1) % LAYERS) for z in range(LAYERS)]]
    steps.append([(z, z + 1) for z in range(stage - 1, LAYERS - 1)])
    if stage == LAYERS - 1:
        steps[1].append((LAYERS - 1, LAYERS - 2))
    pairs = []
    for core in range(2):
        for source, target in steps[core]:
            at, to = [(core * LAYERS + z) * PLANE for z in (source, target)]
            pairs += [(at + i, to + i) for i in range(PLANE)]
    return pairs


def tied(value, after):
    return lax.optimization_barrier((value, *after))[0] if after else value


def fit_kernel(count, flags, *refs):
    pieces, factor = refs[:count], refs[count]
    *before, out = refs[count + 1 :]
    wide = pieces[0].shape[0]
    places = [i * wide for i in range(count)]
    turned = flags[1] * wide
    lead = max(count - PLANE, 0) * wide
    places[1 + lead // wide] = pl.multiple_of(lead + 2 * wide - turned, 32)
    places[2 + lead // wide] = pl.multiple_of(lead + wide + turned, 32)

    @pl.when(flags[0] == 1)
    def _():
        total = lax.dot_general(
            jnp.concatenate([piece[...] for piece in pieces]),
            factor[...],
            (((1,), (1,)), ((), ())),
            preferred_element_type=jnp.float32,
        )
        for i, at in enumerate(places):
            part = total[i * wide : (i + 1) * wide]
            if before:
                part += before[0][pl.ds(at, wide), :]
            out[pl.ds(at, wide), :] = part.astype(out.dtype)

    @pl.when(flags[0] == 0)
    def _():
        out[...] = jnp.zeros(out.shape, out.dtype)


def fit(flags, pieces, factor, part=0, parts=1, before=None, dtype=jnp.bfloat16):
    depth = factor.shape[1] // parts
    wide = sum(piece.shape[0] for piece in pieces)
    rows = factor.shape[0]
    step = min(rows, 256)
    whole = pl.BlockSpec((pieces[0].shape[0], depth), lambda i, flags: (0, part))
    alone = pl.BlockSpec((pieces[0].shape[0], depth), lambda i, flags: (0, 0))
    tile = pl.BlockSpec((wide, step), lambda i, flags: (0, i))
    return pl.pallas_call(
        functools.partial(fit_kernel, len(pieces)),
        out_shape=jax.ShapeDtypeStruct((wide, rows), dtype),
        grid_spec=pltpu.PrefetchScalarGridSpec(
            num_scalar_prefetch=1,
            grid=(rows // step,),
            in_specs=[alone if piece.shape[1] == depth else whole for piece in pieces]
            + [pl.BlockSpec((step, depth), lambda i, flags: (i * flags[0], part))]
            + ([] if before is None else [tile]),
            out_specs=tile,
        ),
        compiler_params=pltpu.CompilerParams(vmem_limit_bytes=40 << 20),
        cost_estimate=pl.CostEstimate(
            flops=2 * wide * depth * rows,
            bytes_accessed=2 * (depth * (wide + rows) + wide * rows),
            transcendentals=0,
        ),
    )(flags, *pieces, factor, *(() if before is None else (before,)))


def shards_stacked(metric_factor, three_centre, occ_energy, virt_energy):
    aux_id = lax.axis_index("aux")
    pair_id = lax.axis_index("pair")
    layer = pair_id // PLANE
    place = pair_id % PLANE
    share_rows = three_centre.shape[1]
    pair_count = LAYERS * PLANE
    pairs_total = share_rows * pair_count
    share_cols = pairs_total // 2
    rows = metric_factor.shape[0]
    own = three_centre.T
    needed = jnp.logical_or(aux_id == 0, layer >= LAYERS // 2)
    crossed = []

    def cross(piece, turn, after=()):
        after = [*crossed[-4:][: max(len(crossed) - 3, 0)][:1], *after]
        crossed.append(lax.ppermute(tied(piece, after), AXES, along(turn)))
        return crossed[-1]

    def spread(piece, after=(), near=None, tie=()):
        near = tied(cross(piece, TURN), tie) if near is None else near
        far = cross(piece, TURN[::-1])
        return [piece, near, far, cross(near, TURN[::-1], after)]

    def climb(piece, stage, after=()):
        return lax.ppermute(tied(piece, after), AXES, climbs(stage))

    flags = jnp.stack([needed, aux_id == 0]).astype(jnp.int32)

    def fitted_of(pieces, *more):
        partial = fit(flags, pieces, metric_factor, *more)
        other = lax.ppermute(partial, "aux", [(0, 1), (1, 0)])
        total = partial.astype(jnp.float32) + other.astype(jnp.float32)
        return partial, total.astype(jnp.bfloat16)

    above_1 = climb(own, 1)
    plane_0 = spread(own)
    above_2 = climb(above_1, 2, plane_0[1:3])
    plane_1 = spread(above_1)
    turning = jnp.logical_and(aux_id == 1, layer == LAYERS - 1)
    above_3 = climb(jnp.where(turning, own, above_2), 3, plane_1[1:2])
    partial_0, fitted_0 = fitted_of(plane_0)
    plane_2 = spread(above_2, tie=[partial_0])
    partial_1, fitted_1 = fitted_of(plane_1)
    near_3 = climb(jnp.where(turning, plane_0[1], plane_2[1]), 3)
    half = own.shape[1] // 2
    far_3 = [cross(above_3[:, :half], TURN[::-1])]
    partial_2, fitted_2 = fitted_of(plane_2[:3])
    near_3 = tied(near_3, [partial_1, partial_2, plane_2[3]])
    far_3.append(climb(jnp.where(turning, plane_0[2], plane_2[2])[:, half:], 3, [near_3]))
    both_3 = [cross(near_3[:, i * half : (i + 1) * half], TURN[::-1]) for i in range(2)]
    both_3[0] = tied(both_3[0], [fitted_0, fitted_1, fitted_2])
    partial_3 = fit(
        flags, [plane_2[3], above_3, near_3, far_3[0], both_3[0]], metric_factor, 0, 2, None, jnp.float32
    )
    both_3[1] = tied(both_3[1], [partial_3])
    fitted_3 = fitted_of([plane_2[3], above_3, near_3, far_3[1], both_3[1]], 1, 2, partial_3)[1]
    fitted = jnp.concatenate([fitted_0, fitted_1, fitted_2, fitted_3])
    blocks = fitted.reshape(pair_count, share_rows, rows)
    ordered = []
    for z in range(LAYERS):
        slot = (layer - z) % LAYERS
        for where in range(PLANE):
            offset = place ^ where
            at = slot * PLANE + offset
            ordered.append(lax.dynamic_index_in_dim(blocks, at, 0, keepdims=False))
    fitted = jnp.concatenate(ordered)
    own_share = lax.dynamic_slice_in_dim(fitted, aux_id * share_cols, share_cols, 0)
    grid = (LAYERS, PLANE, share_rows, rows)
    turned = jnp.swapaxes(fitted.reshape(grid), 0, 1).reshape(fitted.shape)
    partial_tiles = nt_dot(turned, own_share).astype(jnp.bfloat16)
    tiles = partial_tiles.reshape(PLANE, LAYERS, share_rows, share_cols)
    chips = [list(range(z * PLANE, (z + 1) * PLANE)) for z in range(LAYERS)]
    for groups in (chips, [list(group) for group in zip(*chips)]):
        tiles = lax.all_to_all(tiles, "pair", 0, 0, tiled=True, axis_index_groups=groups)
        if groups is chips:
            tiles = jnp.sum(tiles.astype(jnp.float32), axis=0).astype(jnp.bfloat16)
    return outputs(tiles, occ_energy, virt_energy)


def solution(mesh):
    in_specs = (P("pair", "aux"), P("aux", "pair"), P(), P())
    out_specs = (P("pair", "aux"), P())
    stacked = mesh.shape["aux"] == 2 and mesh.shape["pair"] == LAYERS * PLANE
    return jax.shard_map(
        shards_stacked if stacked else shards_any,
        mesh=mesh,
        in_specs=in_specs,
        out_specs=out_specs,
        check_vma=False,
    )
```

profile of v0, /device:TPU:0, one launch (start us, length us, event | category | flops | bytes accessed | tf_op | source)
XLA Modules:
  0.0 273.5 jit_solution(1591363877208568944)
XLA Ops:
  0.6 5.1 %collective-permute-start.4 = (bf16[96,8192]{1,0:T(8,128)(2,1)}, bf16[96,8192]{1,0:T(8,128)(2,1)}, u32[]{:S(2)}, u32[]{:S(2)}) collective-permute-start(bf16[96,8192]{1,0:T(8,128)(2,1)} %bitcast.43), channel_id=1, source_target_pairs={{0,4},{1,5},{2,6},{3,7},{4,8},{5,9},{6,10},{7,11},{8,12},{9,13},{1... | collective-permute-start | bytes 4718600 | tf_op jit(solution)/shard_map/ppermute | solution.py:176
  5.7 3.4 %collective-permute-start.1 = (bf16[96,8192]{1,0:T(8,128)(2,1)}, bf16[96,8192]{1,0:T(8,128)(2,1)S(1)}, u32[]{:S(2)}, u32[]{:S(2)}) collective-permute-start(bf16[96,8192]{1,0:T(8,128)(2,1)} %bitcast.44), channel_id=1, source_target_pairs={{0,2},{1,3},{2,0},{3,1},{4,6},{5,7},{6,4},{7,5},{8,10},{9,11},{10,... | collective-permute-start | bytes 4718600 | tf_op jit(solution)/shard_map/ppermute | solution.py:167
  9.2 3.4 %collective-permute-start = (bf16[96,8192]{1,0:T(8,128)(2,1)}, bf16[96,8192]{1,0:T(8,128)(2,1)}, u32[]{:S(2)}, u32[]{:S(2)}) collective-permute-start(bf16[96,8192]{1,0:T(8,128)(2,1)} %bitcast.45), channel_id=1, source_target_pairs={{0,1},{1,0},{2,3},{3,2},{4,5},{5,4},{6,7},{7,6},{8,9},{9,8},{10,11... | collective-permute-start | bytes 4718600 | tf_op jit(solution)/shard_map/ppermute | solution.py:167
  12.6 27.1 %collective-permute-done.4.refs_0_ = bf16[96,8192]{1,0:T(8,128)(2,1)} collective-permute-done((bf16[96,8192]{1,0:T(8,128)(2,1)}, bf16[96,8192]{1,0:T(8,128)(2,1)}, u32[]{:S(2)}, u32[]{:S(2)}) %collective-permute-start.4) | collective-permute-done | bytes 1572896 | tf_op jit(solution)/shard_map/ppermute | solution.py:176
  39.7 3.4 %collective-permute-start.5 = (bf16[96,8192]{1,0:T(8,128)(2,1)}, bf16[96,8192]{1,0:T(8,128)(2,1)}, u32[]{:S(2)}, u32[]{:S(2)}) collective-permute-start(bf16[96,8192]{1,0:T(8,128)(2,1)} %collective-permute-done.4.refs_0_), channel_id=1, source_target_pairs={{0,1},{1,0},{2,3},{3,2},{4,5},{5,4},{6,7},{7,6},{8,9},{9,8},{10,11... | collective-permute-start | bytes 4718600 | tf_op jit(solution)/shard_map/ppermute | solution.py:167
  44.3 4.4 %collective-permute-start.9 = (bf16[96,8192]{1,0:T(8,128)(2,1)}, bf16[96,8192]{1,0:T(8,128)(2,1)S(1)}, u32[]{:S(2)}, u32[]{:S(2)}) collective-permute-start(bf16[96,8192]{1,0:T(8,128)(2,1)} %collective-permute-done.4.refs_0_), channel_id=1, source_target_pairs={{0,4},{1,5},{2,6},{3,7},{4,8},{5,9},{6,10},{7,11},{8,12},{9,13},{1... | collective-permute-start | bytes 4718600 | tf_op jit(solution)/shard_map/ppermute | solution.py:176
  48.7 3.4 %collective-permute-start.2 = (bf16[96,8192]{1,0:T(8,128)(2,1)}, bf16[96,8192]{1,0:T(8,128)(2,1)}, u32[]{:S(2)}, u32[]{:S(2)}) collective-permute-start(bf16[96,8192]{1,0:T(8,128)(2,1)} %collective-permute-done.refs_1_), channel_id=1, source_target_pairs={{0,2},{1,3},{2,0},{3,1},{4,6},{5,7},{6,4},{7,5},{8,10},{9,11},{10,... | collective-permute-start | bytes 4718600 | tf_op jit(solution)/shard_map/ppermute | solution.py:167
  52.2 2.5 collective-permute-start.6
  54.8 7.5 %collective-permute-done.5.refs_1_ = bf16[96,8192]{1,0:T(8,128)(2,1)} collective-permute-done((bf16[96,8192]{1,0:T(8,128)(2,1)}, bf16[96,8192]{1,0:T(8,128)(2,1)}, u32[]{:S(2)}, u32[]{:S(2)}) %collective-permute-start.5) | collective-permute-done | bytes 1572896 | tf_op jit(solution)/shard_map/ppermute | solution.py:167
  62.3 3.4 %collective-permute-start.7 = (bf16[96,8192]{1,0:T(8,128)(2,1)}, bf16[96,8192]{1,0:T(8,128)(2,1)S(1)}, u32[]{:S(2)}, u32[]{:S(2)}) collective-permute-start(bf16[96,8192]{1,0:T(8,128)(2,1)} %collective-permute-done.5.refs_1_), channel_id=1, source_target_pairs={{0,2},{1,3},{2,0},{3,1},{4,6},{5,7},{6,4},{7,5},{8,10},{9,11},{10,... | collective-permute-start | bytes 4718600 | tf_op jit(solution)/shard_map/ppermute | solution.py:167
  65.7 3.6 %collective-permute-done.9.refs_0_ = bf16[96,8192]{1,0:T(8,128)(2,1)S(1)} collective-permute-done((bf16[96,8192]{1,0:T(8,128)(2,1)}, bf16[96,8192]{1,0:T(8,128)(2,1)S(1)}, u32[]{:S(2)}, u32[]{:S(2)}) %collective-permute-start.9) | collective-permute-done | bytes 1572896 | tf_op jit(solution)/shard_map/ppermute | solution.py:176
  71.3 2.4 collective-permute-start.10
  75.3 15.8 %collective-permute-start.14 = (bf16[96,8192]{1,0:T(8,128)(2,1)S(1)}, bf16[96,8192]{1,0:T(8,128)(2,1)S(1)}, u32[]{:S(2)}, u32[]{:S(2)}) collective-permute-start(bf16[96,8192]{1,0:T(8,128)(2,1)S(1)} %broadcast_select_fusion.1), channel_id=1, source_target_pairs={{0,4},{1,5},{2,6},{3,7},{4,8},{5,9},{6,10},{7,11},{8,12},{9,13},{1... | collective-permute-start | bytes 4718600 | tf_op jit(solution)/shard_map/ppermute | solution.py:176
  91.1 3.4 %collective-permute-start.11 = (bf16[96,8192]{1,0:T(8,128)(2,1)S(1)}, bf16[96,8192]{1,0:T(8,128)(2,1)S(1)}, u32[]{:S(2)}, u32[]{:S(2)}) collective-permute-start(bf16[96,8192]{1,0:T(8,128)(2,1)S(1)} %collective-permute-done.9.refs_0_), channel_id=1, source_target_pairs={{0,2},{1,3},{2,0},{3,1},{4,6},{5,7},{6,4},{7,5},{8,10},{9,11},{10,... | collective-permute-start | bytes 4718600 | tf_op jit(solution)/shard_map/ppermute | solution.py:167
  94.5 11.6 %shard_map.59 = bf16[384,1024]{1,0:T(8,128)(2,1)S(1)} custom-call(s32[2]{0:T(128)S(1)} %add_convert_fusion.4.flags, bf16[96,8192]{1,0:T(8,128)(2,1)S(1)} %bitcast.46, bf16[96,8192]{1,0:T(8,128)(2,1)} %collective-permute-done.refs_1_, bf16[96,8192]{1,0:T(8,128)(2,1)S(1)} %copy-done.2, bf16[96,8192]{1,0:T(8,128)(2,1)} %collective-permute-done.2.refs_3_, ...), custom_call_target="tpu_custom_call" | custom-call | flops 6442450944 | bytes 23855104 | tf_op jit(solution)/shard_map/pallas_call | solution.py:131
  106.2 2.4 collective-permute-start.13
  108.9 4.3 %collective-permute-start.15 = (bf16[96,8192]{1,0:T(8,128)(2,1)S(1)}, bf16[96,8192]{1,0:T(8,128)(2,1)S(1)}, u32[]{:S(2)}, u32[]{:S(2)}) collective-permute-start(bf16[96,8192]{1,0:T(8,128)(2,1)S(1)} %broadcast_select_fusion), channel_id=1, source_target_pairs={{0,4},{1,5},{2,6},{3,7},{4,8},{5,9},{6,10},{7,11},{8,12},{9,13},{1... | collective-permute-start | bytes 4718600 | tf_op jit(solution)/shard_map/ppermute | solution.py:176
  114.4 11.7 %shard_map.60 = bf16[384,1024]{1,0:T(8,128)(2,1)S(1)} custom-call(s32[2]{0:T(128)S(1)} %add_convert_fusion.4.flags, bf16[96,8192]{1,0:T(8,128)(2,1)} %collective-permute-done.4.refs_0_, bf16[96,8192]{1,0:T(8,128)(2,1)} %collective-permute-done.5.refs_1_, bf16[96,8192]{1,0:T(8,128)(2,1)S(1)} %collective-permute-done.6.refs_2_, ...), custom_call_target="tpu_custom_call" | custom-call | flops 6442450944 | bytes 23855104 | tf_op jit(solution)/shard_map/pallas_call | solution.py:131
  127.4 2.4 collective-permute-start.18
  129.8 9.7 %shard_map.61 = bf16[288,1024]{1,0:T(8,128)(2,1)S(1)} custom-call(s32[2]{0:T(128)S(1)} %add_convert_fusion.4.flags, bf16[96,8192]{1,0:T(8,128)(2,1)S(1)} %collective-permute-done.9.refs_0_, bf16[96,8192]{1,0:T(8,128)(2,1)S(1)} %collective-permute-done.10.refs_1_, bf16[96,8192]{1,0:T(8,128)(2,1)S(1)} %collective-permute-done.11.refs_2_, ...), custom_call_target="tpu_custom_call" | custom-call | flops 4831838208 | bytes 22085632 | tf_op jit(solution)/shard_map/pallas_call | solution.py:131
  139.6 25.1 %collective-permute-done.15.refs_2_ = bf16[96,8192]{1,0:T(8,128)(2,1)S(1)} collective-permute-done((bf16[96,8192]{1,0:T(8,128)(2,1)S(1)}, bf16[96,8192]{1,0:T(8,128)(2,1)S(1)}, u32[]{:S(2)}, u32[]{:S(2)}) %collective-permute-start.15) | collective-permute-done | bytes 1572896 | tf_op jit(solution)/shard_map/ppermute | solution.py:176
  168.8 4.1 %collective-permute-start.17 = (bf16[96,4096]{1,0:T(8,128)(2,1)S(1)}, bf16[96,4096]{1,0:T(8,128)(2,1)S(1)}, u32[]{:S(2)}, u32[]{:S(2)}) collective-permute-start(bf16[96,4096]{1,0:T(8,128)(2,1)S(1)} %get-tuple-element.27), channel_id=1, source_target_pairs={{0,2},{1,3},{2,0},{3,1},{4,6},{5,7},{6,4},{7,5},{8,10},{9,11},{10,... | collective-permute-start | bytes 2359304 | tf_op jit(solution)/shard_map/ppermute | solution.py:167
  173.5 5.3 %collective-permute-done.19.refs_4_ = bf16[96,4096]{1,0:T(8,128)(2,1)S(1)} collective-permute-done((bf16[96,4096]{1,0:T(8,128)(2,1)S(1)}, bf16[96,4096]{1,0:T(8,128)(2,1)S(1)}, u32[]{:S(2)}, u32[]{:S(2)}) %collective-permute-start.19) | collective-permute-done | bytes 786464 | tf_op jit(solution)/shard_map/ppermute | solution.py:167
  178.7 7.7 %shard_map.62.refs_6_ = f32[480,1024]{1,0:T(8,128)S(1)} custom-call(s32[2]{0:T(128)S(1)} %add_convert_fusion.4.flags, bf16[96,8192]{1,0:T(8,128)(2,1)S(1)} %collective-permute-done.13.refs_0_, bf16[96,8192]{1,0:T(8,128)(2,1)S(1)} %collective-permute-done.14.refs_1_, bf16[96,8192]{1,0:T(8,128)(2,1)S(1)} %collective-permute-done.15.refs_2_, ...), custom_call_target="tpu_custom_call" | custom-call | flops 4026531840 | bytes 13303808 | tf_op jit(solution)/shard_map/pallas_call | solution.py:131
  187.1 3.7 %collective-permute-done.16.refs_3_ = bf16[96,4096]{1,0:T(8,128)(2,1)S(1)} collective-permute-done((bf16[96,4096]{1,0:T(8,128)(2,1)S(1)}, bf16[96,4096]{1,0:T(8,128)(2,1)S(1)}, u32[]{:S(2)}, u32[]{:S(2)}) %collective-permute-start.16) | collective-permute-done | bytes 786464 | tf_op jit(solution)/shard_map/ppermute | solution.py:176
  190.9 7.7 %shard_map.63 = bf16[480,1024]{1,0:T(8,128)(2,1)S(1)} custom-call(s32[2]{0:T(128)S(1)} %add_convert_fusion.4.flags, bf16[96,8192]{1,0:T(8,128)(2,1)S(1)} %collective-permute-done.13.refs_0_, bf16[96,8192]{1,0:T(8,128)(2,1)S(1)} %collective-permute-done.14.refs_1_, bf16[96,8192]{1,0:T(8,128)(2,1)S(1)} %collective-permute-done.15.refs_2_, ...), custom_call_target="tpu_custom_call" | custom-call | flops 4026531840 | bytes 13303808 | tf_op jit(solution)/shard_map/pallas_call | solution.py:131
  198.8 2.5 collective-permute-done.20
  204.3 2.9 %convolution_convert_fusion = bf16[1536,768]{1,0:T(8,128)(2,1)S(1)} fusion(bf16[1536,1024]{1,0:T(8,128)(2,1)S(1)} %bitcast.64, bf16[1536,1024]{1,0:T(8,128)(2,1)S(1)} %bitcast_dynamic-update-slice_fusion, s32[]{:T(128)S(6)} %select_n.125), kind=kOutput, calls=%fused_computation | convolution fusion | flops 2417098752 | bytes 7077892 | tf_op jit(solution)/shard_map/dot_general | solution.py:23
  207.2 31.3 %all_to_all.15 = bf16[4,4,96,768]{3,2,1,0:T(8,128)(2,1)S(1)} all-to-all(bf16[4,4,96,768]{3,2,1,0:T(8,128)(2,1)S(1)} %bitcast.65), channel_id=1, replica_groups={{0,1,2,3},{4,5,6,7},{8,9,10,11},{12,13,14,15},{16,17,18,19},{20,21,22,2..., dimensions={0} | all-to-all | bytes 4718592 | tf_op jit(solution)/shard_map/all_to_all | solution.py:225
  239.8 3.9 %all-to-all-start.1 = ((bf16[4,96,768]{2,1,0:T(8,128)(2,1)}), bf16[4,96,768]{2,1,0:T(8,128)(2,1)S(1)}, u32[]{:S(2)}, u32[]{:S(2)}) async-start(bf16[4,96,768]{2,1,0:T(8,128)(2,1)} %reduce_sum.39), calls=%async_computation.1 | async-start | bytes 1179648 | tf_op jit(solution)/shard_map/all_to_all | solution.py:225
  244.0 14.7 %all-to-all-done.1 = bf16[4,96,768]{2,1,0:T(8,128)(2,1)S(1)} async-done(((bf16[4,96,768]{2,1,0:T(8,128)(2,1)}), bf16[4,96,768]{2,1,0:T(8,128)(2,1)S(1)}, u32[]{:S(2)}, u32[]{:S(2)}) %all-to-all-start.1) | async-done | bytes 589856 | tf_op jit(solution)/shard_map/all_to_all | solution.py:225
  260.8 10.2 %all_to_all.16 = f32[32,8,128]{2,1,0:T(8,128)S(1)} all-to-all(f32[32,8,128]{2,1,0:T(8,128)S(1)} %broadcast_in_dim.2), channel_id=1, replica_groups=mesh['aux'=2,'pair'=16] {'aux','pair'}, dimensions={0} | all-to-all | bytes 262144 | tf_op jit(solution)/shard_map/all_to_all | solution.py:19
  (69 shorter events, 20.3 us)
Async XLA Ops:
  0.6 93.9 %copy-start = (bf16[8192,96]{0,1:T(8,128)(2,1)S(1)}, bf16[8192,96]{0,1:T(8,128)(2,1)}, u32[]{:S(2)}) copy-start(bf16[8192,96]{0,1:T(8,128)(2,1)} %param.5) | copy-start | bytes 4718596
  0.6 39.0 %collective-permute-start.4 = (bf16[96,8192]{1,0:T(8,128)(2,1)}, bf16[96,8192]{1,0:T(8,128)(2,1)}, u32[]{:S(2)}, u32[]{:S(2)}) collective-permute-start(bf16[96,8192]{1,0:T(8,128)(2,1)} %bitcast.43), channel_id=1, source_target_pairs={{0,4},{1,5},{2,6},{3,7},{4,8},{5,9},{6,10},{7,11},{8,12},{9,13},{1... | collective-permute-start | bytes 4718600 | tf_op jit(solution)/shard_map/ppermute | solution.py:176
  5.7 37.3 %collective-permute-start.1 = (bf16[96,8192]{1,0:T(8,128)(2,1)}, bf16[96,8192]{1,0:T(8,128)(2,1)S(1)}, u32[]{:S(2)}, u32[]{:S(2)}) collective-permute-start(bf16[96,8192]{1,0:T(8,128)(2,1)} %bitcast.44), channel_id=1, source_target_pairs={{0,2},{1,3},{2,0},{3,1},{4,6},{5,7},{6,4},{7,5},{8,10},{9,11},{10,... | collective-permute-start | bytes 4718600 | tf_op jit(solution)/shard_map/ppermute | solution.py:167
  9.2 35.1 %collective-permute-start = (bf16[96,8192]{1,0:T(8,128)(2,1)}, bf16[96,8192]{1,0:T(8,128)(2,1)}, u32[]{:S(2)}, u32[]{:S(2)}) collective-permute-start(bf16[96,8192]{1,0:T(8,128)(2,1)} %bitcast.45), channel_id=1, source_target_pairs={{0,1},{1,0},{2,3},{3,2},{4,5},{5,4},{6,7},{7,6},{8,9},{9,8},{10,11... | collective-permute-start | bytes 4718600 | tf_op jit(solution)/shard_map/ppermute | solution.py:167
  39.7 22.6 %collective-permute-start.5 = (bf16[96,8192]{1,0:T(8,128)(2,1)}, bf16[96,8192]{1,0:T(8,128)(2,1)}, u32[]{:S(2)}, u32[]{:S(2)}) collective-permute-start(bf16[96,8192]{1,0:T(8,128)(2,1)} %collective-permute-done.4.refs_0_), channel_id=1, source_target_pairs={{0,1},{1,0},{2,3},{3,2},{4,5},{5,4},{6,7},{7,6},{8,9},{9,8},{10,11... | collective-permute-start | bytes 4718600 | tf_op jit(solution)/shard_map/ppermute | solution.py:167
  43.1 1.2 copy-start.1
  44.3 25.0 %collective-permute-start.9 = (bf16[96,8192]{1,0:T(8,128)(2,1)}, bf16[96,8192]{1,0:T(8,128)(2,1)S(1)}, u32[]{:S(2)}, u32[]{:S(2)}) collective-permute-start(bf16[96,8192]{1,0:T(8,128)(2,1)} %collective-permute-done.4.refs_0_), channel_id=1, source_target_pairs={{0,4},{1,5},{2,6},{3,7},{4,8},{5,9},{6,10},{7,11},{8,12},{9,13},{1... | collective-permute-start | bytes 4718600 | tf_op jit(solution)/shard_map/ppermute | solution.py:176
  48.7 22.6 %collective-permute-start.2 = (bf16[96,8192]{1,0:T(8,128)(2,1)}, bf16[96,8192]{1,0:T(8,128)(2,1)}, u32[]{:S(2)}, u32[]{:S(2)}) collective-permute-start(bf16[96,8192]{1,0:T(8,128)(2,1)} %collective-permute-done.refs_1_), channel_id=1, source_target_pairs={{0,2},{1,3},{2,0},{3,1},{4,6},{5,7},{6,4},{7,5},{8,10},{9,11},{10,... | collective-permute-start | bytes 4718600 | tf_op jit(solution)/shard_map/ppermute | solution.py:167
  52.1 42.4 %copy-start.2 = (bf16[96,8192]{1,0:T(8,128)(2,1)S(1)}, bf16[96,8192]{1,0:T(8,128)(2,1)}, u32[]{:S(2)}) copy-start(bf16[96,8192]{1,0:T(8,128)(2,1)} %copy-done.1) | copy-start | bytes 4718596
  52.2 54.0 %collective-permute-start.6 = (bf16[96,8192]{1,0:T(8,128)(2,1)}, bf16[96,8192]{1,0:T(8,128)(2,1)S(1)}, u32[]{:S(2)}, u32[]{:S(2)}) collective-permute-start(bf16[96,8192]{1,0:T(8,128)(2,1)} %collective-permute-done.4.refs_0_), channel_id=1, source_target_pairs={{0,2},{1,3},{2,0},{3,1},{4,6},{5,7},{6,4},{7,5},{8,10},{9,11},{10,... | collective-permute-start | bytes 4718600 | tf_op jit(solution)/shard_map/ppermute | solution.py:167
  62.3 52.1 %collective-permute-start.7 = (bf16[96,8192]{1,0:T(8,128)(2,1)}, bf16[96,8192]{1,0:T(8,128)(2,1)S(1)}, u32[]{:S(2)}, u32[]{:S(2)}) collective-permute-start(bf16[96,8192]{1,0:T(8,128)(2,1)} %collective-permute-done.5.refs_1_), channel_id=1, source_target_pairs={{0,2},{1,3},{2,0},{3,1},{4,6},{5,7},{6,4},{7,5},{8,10},{9,11},{10,... | collective-permute-start | bytes 4718600 | tf_op jit(solution)/shard_map/ppermute | solution.py:167
  71.3 34.8 %collective-permute-start.10 = (bf16[96,8192]{1,0:T(8,128)(2,1)S(1)}, bf16[96,8192]{1,0:T(8,128)(2,1)S(1)}, u32[]{:S(2)}, u32[]{:S(2)}) collective-permute-start(bf16[96,8192]{1,0:T(8,128)(2,1)S(1)} %collective-permute-done.9.refs_0_), channel_id=1, source_target_pairs={{0,1},{1,0},{2,3},{3,2},{4,5},{5,4},{6,7},{7,6},{8,9},{9,8},{10,11... | collective-permute-start | bytes 4718600 | tf_op jit(solution)/shard_map/ppermute | solution.py:167
  75.3 52.0 %collective-permute-start.14 = (bf16[96,8192]{1,0:T(8,128)(2,1)S(1)}, bf16[96,8192]{1,0:T(8,128)(2,1)S(1)}, u32[]{:S(2)}, u32[]{:S(2)}) collective-permute-start(bf16[96,8192]{1,0:T(8,128)(2,1)S(1)} %broadcast_select_fusion.1), channel_id=1, source_target_pairs={{0,4},{1,5},{2,6},{3,7},{4,8},{5,9},{6,10},{7,11},{8,12},{9,13},{1... | collective-permute-start | bytes 4718600 | tf_op jit(solution)/shard_map/ppermute | solution.py:176
  91.1 38.7 %collective-permute-start.11 = (bf16[96,8192]{1,0:T(8,128)(2,1)S(1)}, bf16[96,8192]{1,0:T(8,128)(2,1)S(1)}, u32[]{:S(2)}, u32[]{:S(2)}) collective-permute-start(bf16[96,8192]{1,0:T(8,128)(2,1)S(1)} %collective-permute-done.9.refs_0_), channel_id=1, source_target_pairs={{0,2},{1,3},{2,0},{3,1},{4,6},{5,7},{6,4},{7,5},{8,10},{9,11},{10,... | collective-permute-start | bytes 4718600 | tf_op jit(solution)/shard_map/ppermute | solution.py:167
  106.1 2.7 %collective-permute-start.3 = (bf16[384,1024]{1,0:T(8,128)(2,1)S(1)}, bf16[384,1024]{1,0:T(8,128)(2,1)S(1)}, u32[]{:S(2)}, u32[]{:S(2)}) collective-permute-start(bf16[384,1024]{1,0:T(8,128)(2,1)S(1)} %shard_map.59), channel_id=1, source_target_pairs={{0,16},{16,0},{1,17},{17,1},{2,18},{18,2},{3,19},{19,3},{4,20},{20... | collective-permute-start | bytes 2359304 | tf_op jit(solution)/shard_map/ppermute | solution.py:182
  106.2 33.3 %collective-permute-start.13 = (bf16[96,8192]{1,0:T(8,128)(2,1)S(1)}, bf16[96,8192]{1,0:T(8,128)(2,1)S(1)}, u32[]{:S(2)}, u32[]{:S(2)}) collective-permute-start(bf16[96,8192]{1,0:T(8,128)(2,1)S(1)} %collective-permute-done.10.refs_1_), channel_id=1, source_target_pairs={{0,2},{1,3},{2,0},{3,1},{4,6},{5,7},{6,4},{7,5},{8,10},{9,11},{10,... | collective-permute-start | bytes 4718600 | tf_op jit(solution)/shard_map/ppermute | solution.py:167
  108.9 55.8 %collective-permute-start.15 = (bf16[96,8192]{1,0:T(8,128)(2,1)S(1)}, bf16[96,8192]{1,0:T(8,128)(2,1)S(1)}, u32[]{:S(2)}, u32[]{:S(2)}) collective-permute-start(bf16[96,8192]{1,0:T(8,128)(2,1)S(1)} %broadcast_select_fusion), channel_id=1, source_target_pairs={{0,4},{1,5},{2,6},{3,7},{4,8},{5,9},{6,10},{7,11},{8,12},{9,13},{1... | collective-permute-start | bytes 4718600 | tf_op jit(solution)/shard_map/ppermute | solution.py:176
  126.0 47.1 %collective-permute-start.8 = (bf16[384,1024]{1,0:T(8,128)(2,1)S(1)}, bf16[384,1024]{1,0:T(8,128)(2,1)S(1)}, u32[]{:S(2)}, u32[]{:S(2)}) collective-permute-start(bf16[384,1024]{1,0:T(8,128)(2,1)S(1)} %shard_map.60), channel_id=1, source_target_pairs={{0,16},{16,0},{1,17},{17,1},{2,18},{18,2},{3,19},{19,3},{4,20},{20... | collective-permute-start | bytes 2359304 | tf_op jit(solution)/shard_map/ppermute | solution.py:182
  127.4 51.3 %collective-permute-start.18 = (bf16[96,4096]{1,0:T(8,128)(2,1)S(1)}, bf16[96,4096]{1,0:T(8,128)(2,1)S(1)}, u32[]{:S(2)}, u32[]{:S(2)}) collective-permute-start(bf16[96,4096]{1,0:T(8,128)(2,1)S(1)} %slice.22), channel_id=1, source_target_pairs={{0,2},{1,3},{2,0},{3,1},{4,6},{5,7},{6,4},{7,5},{8,10},{9,11},{10,... | collective-permute-start | bytes 2359304 | tf_op jit(solution)/shard_map/ppermute | solution.py:167
  139.5 29.3 %collective-permute-start.12 = (bf16[288,1024]{1,0:T(8,128)(2,1)S(1)}, bf16[288,1024]{1,0:T(8,128)(2,1)S(1)}, u32[]{:S(2)}, u32[]{:S(2)}) collective-permute-start(bf16[288,1024]{1,0:T(8,128)(2,1)S(1)} %shard_map.61), channel_id=1, source_target_pairs={{0,16},{16,0},{1,17},{17,1},{2,18},{18,2},{3,19},{19,3},{4,20},{20... | collective-permute-start | bytes 1769480 | tf_op jit(solution)/shard_map/ppermute | solution.py:182
  164.8 13.9 %collective-permute-start.19 = (bf16[96,4096]{1,0:T(8,128)(2,1)S(1)}, bf16[96,4096]{1,0:T(8,128)(2,1)S(1)}, u32[]{:S(2)}, u32[]{:S(2)}) collective-permute-start(bf16[96,4096]{1,0:T(8,128)(2,1)S(1)} %get-tuple-element.29), channel_id=1, source_target_pairs={{0,2},{1,3},{2,0},{3,1},{4,6},{5,7},{6,4},{7,5},{8,10},{9,11},{10,... | collective-permute-start | bytes 2359304 | tf_op jit(solution)/shard_map/ppermute | solution.py:167
  166.9 24.0 %collective-permute-start.16 = (bf16[96,4096]{1,0:T(8,128)(2,1)S(1)}, bf16[96,4096]{1,0:T(8,128)(2,1)S(1)}, u32[]{:S(2)}, u32[]{:S(2)}) collective-permute-start(bf16[96,4096]{1,0:T(8,128)(2,1)S(1)} %slice_select_fusion), channel_id=1, source_target_pairs={{0,4},{1,5},{2,6},{3,7},{4,8},{5,9},{6,10},{7,11},{8,12},{9,13},{1... | collective-permute-start | bytes 2359304 | tf_op jit(solution)/shard_map/ppermute | solution.py:176
  168.8 18.4 %collective-permute-start.17 = (bf16[96,4096]{1,0:T(8,128)(2,1)S(1)}, bf16[96,4096]{1,0:T(8,128)(2,1)S(1)}, u32[]{:S(2)}, u32[]{:S(2)}) collective-permute-start(bf16[96,4096]{1,0:T(8,128)(2,1)S(1)} %get-tuple-element.27), channel_id=1, source_target_pairs={{0,2},{1,3},{2,0},{3,1},{4,6},{5,7},{6,4},{7,5},{8,10},{9,11},{10,... | collective-permute-start | bytes 2359304 | tf_op jit(solution)/shard_map/ppermute | solution.py:167
  198.6 4.3 %copy-start.3 = (bf16[384,1024]{1,0:T(8,128)(2,1)S(1)}, bf16[384,1024]{1,0:T(8,128)(2,1)}, u32[]{:S(2)}) copy-start(bf16[384,1024]{1,0:T(8,128)(2,1)} %add_convert_fusion.2) | copy-start | bytes 2359300
  198.6 2.8 %collective-permute-start.20 = (bf16[480,1024]{1,0:T(8,128)(2,1)S(1)}, bf16[480,1024]{1,0:T(8,128)(2,1)}, u32[]{:S(2)}, u32[]{:S(2)}) collective-permute-start(bf16[480,1024]{1,0:T(8,128)(2,1)S(1)} %shard_map.63), channel_id=1, source_target_pairs={{0,16},{16,0},{1,17},{17,1},{2,18},{18,2},{3,19},{19,3},{4,20},{20... | collective-permute-start | bytes 2949128 | tf_op jit(solution)/shard_map/ppermute | solution.py:182
  238.5 5.3 %copy-start.4 = (f32[768]{0:T(1024)S(1)}, f32[768]{0:T(1024)}, u32[]{:S(2)}) copy-start(f32[768]{0:T(1024)} %param.7) | copy-start | bytes 9220
  238.5 5.3 %copy-start.5 = (f32[2]{0:T(128)S(1)}, f32[2]{0:T(128)}, u32[]{:S(2)}) copy-start(f32[2]{0:T(128)} %param.6) | copy-start | bytes 28
  239.8 18.9 %all-to-all-start.1 = ((bf16[4,96,768]{2,1,0:T(8,128)(2,1)}), bf16[4,96,768]{2,1,0:T(8,128)(2,1)S(1)}, u32[]{:S(2)}, u32[]{:S(2)}) async-start(bf16[4,96,768]{2,1,0:T(8,128)(2,1)} %reduce_sum.39), calls=%async_computation.1 | async-start | bytes 1179648 | tf_op jit(solution)/shard_map/all_to_all | solution.py:225
where the time goes:
time: 275 us; the launch traced here: 273 us
  waiting for transfers between devices  93.4 us (34%)
  starting transfers between devices  71.9 us (26%)
  Pallas kernels  48.3 us (18%)
  blocking collectives  41.5 us (15%)
  other arithmetic  9.24 us (3%)
  between operations  3.16 us (1%)
  local copies, waits for them, and re-layouts  3.01 us (1%)
  matrix products  2.9 us (1%)
    ppermute x5, waiting for transfers between devices, climb(): return lax.ppermute(tied(piece, after), AXES, climbs(stage))  60.7 us
    pallas_call x5, Pallas kernels, fit(): pl.pallas_call(functools.partial(fit_kernel, len(pieces)), out_shape=jax....  48.3 us
    ppermute x12, starting transfers between devices, cross(): crossed.append(lax.ppermute(tied(piece, after), AXES, along(turn)))  36.3 us
    ppermute x5, starting transfers between devices, climb(): return lax.ppermute(tied(piece, after), AXES, climbs(stage))  31.4 us
    all_to_all x1, blocking collectives, shards_stacked(): lax.all_to_all(tiles, 'pair', 0, 0, tiled=True, axis_index_groups=groups)  31.3 us
    ppermute x12, waiting for transfers between devices, cross(): crossed.append(lax.ppermute(tied(piece, after), AXES, along(turn)))  15.5 us
    all_to_all x1, waiting for transfers between devices, shards_stacked(): lax.all_to_all(tiles, 'pair', 0, 0, tiled=True, axis_index_groups=groups)  14.7 us
    all_to_all x1, blocking collectives, total_of(): return jnp.sum(lax.all_to_all(sent, axes, 0, 0, tiled=True)[:, 0, 0])  10.2 us
  transfers between devices with their start and end apart: 22, of which 11 were waited for; matrix products, arithmetic and copies ran while one was open for 2% of the time, Pallas kernels for 15%

commit v1 on v0

--- a/solution.py
+++ b/solution.py
@@ -15,7 +15,7 @@
 
 def total_of(value, axes):
     count = lax.axis_size(axes)
-    sent = jnp.broadcast_to(value, (count, 8, 128))
+    sent = jnp.broadcast_to(value, (count, 1, 128))
     return jnp.sum(lax.all_to_all(sent, axes, 0, 0, tiled=True)[:, 0, 0])
 
 
@@ -221,10 +221,15 @@
     partial_tiles = nt_dot(turned, own_share).astype(jnp.bfloat16)
     tiles = partial_tiles.reshape(PLANE, LAYERS, share_rows, share_cols)
     chips = [list(range(z * PLANE, (z + 1) * PLANE)) for z in range(LAYERS)]
-    for groups in (chips, [list(group) for group in zip(*chips)]):
-        tiles = lax.all_to_all(tiles, "pair", 0, 0, tiled=True, axis_index_groups=groups)
-        if groups is chips:
-            tiles = jnp.sum(tiles.astype(jnp.float32), axis=0).astype(jnp.bfloat16)
+    tiles = lax.all_to_all(tiles, "pair", 0, 0, tiled=True, axis_index_groups=chips)
+    sums = jnp.sum(tiles.astype(jnp.float32), axis=0)
+    columns = [list(group) for group in zip(*chips)]
+    tiles = lax.all_to_all(
+        sums.astype(jnp.bfloat16), "pair", 0, 0, tiled=True, axis_index_groups=columns
+    )
+    own_sum = lax.dynamic_index_in_dim(sums, layer, 0, keepdims=False)
+    is_own = (jnp.arange(LAYERS) == layer)[:, None, None]
+    tiles = jnp.where(is_own, own_sum[None], tiles.astype(jnp.float32))
     return outputs(tiles, occ_energy, virt_energy)
 
 

time: 275 us -> 274 us (level)
  no operation moved by 1% of the time
where the time goes in v1:
time: 274 us; the launch traced here: 273 us
  waiting for transfers between devices  93.4 us (34%)
  starting transfers between devices  71.9 us (26%)
  Pallas kernels  48.3 us (18%)
  blocking collectives  40.7 us (15%)
  other arithmetic  9.28 us (3%)
  between operations  3.18 us (1%)
  local copies, waits for them, and re-layouts  3.03 us (1%)
  matrix products  2.9 us (1%)
    ppermute x5, waiting for transfers between devices, climb(): return lax.ppermute(tied(piece, after), AXES, climbs(stage))  60.7 us
    pallas_call x5, Pallas kernels, fit(): pl.pallas_call(functools.partial(fit_kernel, len(pieces)), out_shape=jax....  48.3 us
    ppermute x12, starting transfers between devices, cross(): crossed.append(lax.ppermute(tied(piece, after), AXES, along(turn)))  36.3 us
    ppermute x5, starting transfers between devices, climb(): return lax.ppermute(tied(piece, after), AXES, climbs(stage))  31.4 us
    all_to_all x1, blocking collectives, shards_stacked(): lax.all_to_all(tiles, 'pair', 0, 0, tiled=True, axis_index_groups=chips)  31.3 us
    ppermute x12, waiting for transfers between devices, cross(): crossed.append(lax.ppermute(tied(piece, after), AXES, along(turn)))  15.5 us
    all_to_all x1, waiting for transfers between devices, shards_stacked(): lax.all_to_all(sums.astype(jnp.bfloat16), 'pair', 0, 0, tiled=True, axis_...  14.7 us
    all_to_all x1, blocking collectives, total_of(): return jnp.sum(lax.all_to_all(sent, axes, 0, 0, tiled=True)[:, 0, 0])  9.46 us
  transfers between devices with their start and end apart: 22, of which 11 were waited for; matrix products, arithmetic and copies ran while one was open for 2% of the time, Pallas kernels for 15%

profile of v1, /device:TPU:0, one launch (start us, length us, event | category | flops | bytes accessed | tf_op | source)
XLA Modules:
  0.0 272.7 jit_solution(7170996881937137772)
XLA Ops:
  0.6 5.1 %collective-permute-start.4 = (bf16[96,8192]{1,0:T(8,128)(2,1)}, bf16[96,8192]{1,0:T(8,128)(2,1)}, u32[]{:S(2)}, u32[]{:S(2)}) collective-permute-start(bf16[96,8192]{1,0:T(8,128)(2,1)} %bitcast.45), channel_id=1, source_target_pairs={{0,4},{1,5},{2,6},{3,7},{4,8},{5,9},{6,10},{7,11},{8,12},{9,13},{1... | collective-permute-start | bytes 4718600 | tf_op jit(solution)/shard_map/ppermute | solution.py:176
  5.7 3.4 %collective-permute-start.1 = (bf16[96,8192]{1,0:T(8,128)(2,1)}, bf16[96,8192]{1,0:T(8,128)(2,1)S(1)}, u32[]{:S(2)}, u32[]{:S(2)}) collective-permute-start(bf16[96,8192]{1,0:T(8,128)(2,1)} %bitcast.46), channel_id=1, source_target_pairs={{0,2},{1,3},{2,0},{3,1},{4,6},{5,7},{6,4},{7,5},{8,10},{9,11},{10,... | collective-permute-start | bytes 4718600 | tf_op jit(solution)/shard_map/ppermute | solution.py:167
  9.2 3.4 %collective-permute-start = (bf16[96,8192]{1,0:T(8,128)(2,1)}, bf16[96,8192]{1,0:T(8,128)(2,1)}, u32[]{:S(2)}, u32[]{:S(2)}) collective-permute-start(bf16[96,8192]{1,0:T(8,128)(2,1)} %bitcast.47), channel_id=1, source_target_pairs={{0,1},{1,0},{2,3},{3,2},{4,5},{5,4},{6,7},{7,6},{8,9},{9,8},{10,11... | collective-permute-start | bytes 4718600 | tf_op jit(solution)/shard_map/ppermute | solution.py:167
  12.6 27.1 %collective-permute-done.4.refs_0_ = bf16[96,8192]{1,0:T(8,128)(2,1)} collective-permute-done((bf16[96,8192]{1,0:T(8,128)(2,1)}, bf16[96,8192]{1,0:T(8,128)(2,1)}, u32[]{:S(2)}, u32[]{:S(2)}) %collective-permute-start.4) | collective-permute-done | bytes 1572896 | tf_op jit(solution)/shard_map/ppermute | solution.py:176
  39.7 3.4 %collective-permute-start.5 = (bf16[96,8192]{1,0:T(8,128)(2,1)}, bf16[96,8192]{1,0:T(8,128)(2,1)}, u32[]{:S(2)}, u32[]{:S(2)}) collective-permute-start(bf16[96,8192]{1,0:T(8,128)(2,1)} %collective-permute-done.4.refs_0_), channel_id=1, source_target_pairs={{0,1},{1,0},{2,3},{3,2},{4,5},{5,4},{6,7},{7,6},{8,9},{9,8},{10,11... | collective-permute-start | bytes 4718600 | tf_op jit(solution)/shard_map/ppermute | solution.py:167
  44.3 4.4 %collective-permute-start.9 = (bf16[96,8192]{1,0:T(8,128)(2,1)}, bf16[96,8192]{1,0:T(8,128)(2,1)S(1)}, u32[]{:S(2)}, u32[]{:S(2)}) collective-permute-start(bf16[96,8192]{1,0:T(8,128)(2,1)} %collective-permute-done.4.refs_0_), channel_id=1, source_target_pairs={{0,4},{1,5},{2,6},{3,7},{4,8},{5,9},{6,10},{7,11},{8,12},{9,13},{1... | collective-permute-start | bytes 4718600 | tf_op jit(solution)/shard_map/ppermute | solution.py:176
  48.7 3.4 %collective-permute-start.2 = (bf16[96,8192]{1,0:T(8,128)(2,1)}, bf16[96,8192]{1,0:T(8,128)(2,1)}, u32[]{:S(2)}, u32[]{:S(2)}) collective-permute-start(bf16[96,8192]{1,0:T(8,128)(2,1)} %collective-permute-done.refs_1_), channel_id=1, source_target_pairs={{0,2},{1,3},{2,0},{3,1},{4,6},{5,7},{6,4},{7,5},{8,10},{9,11},{10,... | collective-permute-start | bytes 4718600 | tf_op jit(solution)/shard_map/ppermute | solution.py:167
  52.2 2.5 collective-permute-start.6
  54.8 7.5 %collective-permute-done.5.refs_1_ = bf16[96,8192]{1,0:T(8,128)(2,1)} collective-permute-done((bf16[96,8192]{1,0:T(8,128)(2,1)}, bf16[96,8192]{1,0:T(8,128)(2,1)}, u32[]{:S(2)}, u32[]{:S(2)}) %collective-permute-start.5) | collective-permute-done | bytes 1572896 | tf_op jit(solution)/shard_map/ppermute | solution.py:167
  62.3 3.4 %collective-permute-start.7 = (bf16[96,8192]{1,0:T(8,128)(2,1)}, bf16[96,8192]{1,0:T(8,128)(2,1)S(1)}, u32[]{:S(2)}, u32[]{:S(2)}) collective-permute-start(bf16[96,8192]{1,0:T(8,128)(2,1)} %collective-permute-done.5.refs_1_), channel_id=1, source_target_pairs={{0,2},{1,3},{2,0},{3,1},{4,6},{5,7},{6,4},{7,5},{8,10},{9,11},{10,... | collective-permute-start | bytes 4718600 | tf_op jit(solution)/shard_map/ppermute | solution.py:167
  65.7 3.6 %collective-permute-done.9.refs_0_ = bf16[96,8192]{1,0:T(8,128)(2,1)S(1)} collective-permute-done((bf16[96,8192]{1,0:T(8,128)(2,1)}, bf16[96,8192]{1,0:T(8,128)(2,1)S(1)}, u32[]{:S(2)}, u32[]{:S(2)}) %collective-permute-start.9) | collective-permute-done | bytes 1572896 | tf_op jit(solution)/shard_map/ppermute | solution.py:176
  71.3 2.4 collective-permute-start.10
  75.3 15.8 %collective-permute-start.14 = (bf16[96,8192]{1,0:T(8,128)(2,1)S(1)}, bf16[96,8192]{1,0:T(8,128)(2,1)S(1)}, u32[]{:S(2)}, u32[]{:S(2)}) collective-permute-start(bf16[96,8192]{1,0:T(8,128)(2,1)S(1)} %broadcast_select_fusion.1), channel_id=1, source_target_pairs={{0,4},{1,5},{2,6},{3,7},{4,8},{5,9},{6,10},{7,11},{8,12},{9,13},{1... | collective-permute-start | bytes 4718600 | tf_op jit(solution)/shard_map/ppermute | solution.py:176
  91.1 3.4 %collective-permute-start.11 = (bf16[96,8192]{1,0:T(8,128)(2,1)S(1)}, bf16[96,8192]{1,0:T(8,128)(2,1)S(1)}, u32[]{:S(2)}, u32[]{:S(2)}) collective-permute-start(bf16[96,8192]{1,0:T(8,128)(2,1)S(1)} %collective-permute-done.9.refs_0_), channel_id=1, source_target_pairs={{0,2},{1,3},{2,0},{3,1},{4,6},{5,7},{6,4},{7,5},{8,10},{9,11},{10,... | collective-permute-start | bytes 4718600 | tf_op jit(solution)/shard_map/ppermute | solution.py:167
  94.5 11.6 %shard_map.59 = bf16[384,1024]{1,0:T(8,128)(2,1)S(1)} custom-call(s32[2]{0:T(128)S(1)} %add_convert_fusion.4.flags, bf16[96,8192]{1,0:T(8,128)(2,1)S(1)} %bitcast.48, bf16[96,8192]{1,0:T(8,128)(2,1)} %collective-permute-done.refs_1_, bf16[96,8192]{1,0:T(8,128)(2,1)S(1)} %copy-done.2, bf16[96,8192]{1,0:T(8,128)(2,1)} %collective-permute-done.2.refs_3_, ...), custom_call_target="tpu_custom_call" | custom-call | flops 6442450944 | bytes 23855104 | tf_op jit(solution)/shard_map/pallas_call | solution.py:131
  106.2 2.4 collective-permute-start.13
  108.9 4.3 %collective-permute-start.15 = (bf16[96,8192]{1,0:T(8,128)(2,1)S(1)}, bf16[96,8192]{1,0:T(8,128)(2,1)S(1)}, u32[]{:S(2)}, u32[]{:S(2)}) collective-permute-start(bf16[96,8192]{1,0:T(8,128)(2,1)S(1)} %broadcast_select_fusion), channel_id=1, source_target_pairs={{0,4},{1,5},{2,6},{3,7},{4,8},{5,9},{6,10},{7,11},{8,12},{9,13},{1... | collective-permute-start | bytes 4718600 | tf_op jit(solution)/shard_map/ppermute | solution.py:176
  114.4 11.7 %shard_map.60 = bf16[384,1024]{1,0:T(8,128)(2,1)S(1)} custom-call(s32[2]{0:T(128)S(1)} %add_convert_fusion.4.flags, bf16[96,8192]{1,0:T(8,128)(2,1)} %collective-permute-done.4.refs_0_, bf16[96,8192]{1,0:T(8,128)(2,1)} %collective-permute-done.5.refs_1_, bf16[96,8192]{1,0:T(8,128)(2,1)S(1)} %collective-permute-done.6.refs_2_, ...), custom_call_target="tpu_custom_call" | custom-call | flops 6442450944 | bytes 23855104 | tf_op jit(solution)/shard_map/pallas_call | solution.py:131
  127.4 2.4 collective-permute-start.18
  129.8 9.7 %shard_map.61 = bf16[288,1024]{1,0:T(8,128)(2,1)S(1)} custom-call(s32[2]{0:T(128)S(1)} %add_convert_fusion.4.flags, bf16[96,8192]{1,0:T(8,128)(2,1)S(1)} %collective-permute-done.9.refs_0_, bf16[96,8192]{1,0:T(8,128)(2,1)S(1)} %collective-permute-done.10.refs_1_, bf16[96,8192]{1,0:T(8,128)(2,1)S(1)} %collective-permute-done.11.refs_2_, ...), custom_call_target="tpu_custom_call" | custom-call | flops 4831838208 | bytes 22085632 | tf_op jit(solution)/shard_map/pallas_call | solution.py:131
  139.6 25.1 %collective-permute-done.15.refs_2_ = bf16[96,8192]{1,0:T(8,128)(2,1)S(1)} collective-permute-done((bf16[96,8192]{1,0:T(8,128)(2,1)S(1)}, bf16[96,8192]{1,0:T(8,128)(2,1)S(1)}, u32[]{:S(2)}, u32[]{:S(2)}) %collective-permute-start.15) | collective-permute-done | bytes 1572896 | tf_op jit(solution)/shard_map/ppermute | solution.py:176
  168.8 4.1 %collective-permute-start.17 = (bf16[96,4096]{1,0:T(8,128)(2,1)S(1)}, bf16[96,4096]{1,0:T(8,128)(2,1)S(1)}, u32[]{:S(2)}, u32[]{:S(2)}) collective-permute-start(bf16[96,4096]{1,0:T(8,128)(2,1)S(1)} %get-tuple-element.27), channel_id=1, source_target_pairs={{0,2},{1,3},{2,0},{3,1},{4,6},{5,7},{6,4},{7,5},{8,10},{9,11},{10,... | collective-permute-start | bytes 2359304 | tf_op jit(solution)/shard_map/ppermute | solution.py:167
  173.5 5.3 %collective-permute-done.19.refs_4_ = bf16[96,4096]{1,0:T(8,128)(2,1)S(1)} collective-permute-done((bf16[96,4096]{1,0:T(8,128)(2,1)S(1)}, bf16[96,4096]{1,0:T(8,128)(2,1)S(1)}, u32[]{:S(2)}, u32[]{:S(2)}) %collective-permute-start.19) | collective-permute-done | bytes 786464 | tf_op jit(solution)/shard_map/ppermute | solution.py:167
  178.7 7.7 %shard_map.62.refs_6_ = f32[480,1024]{1,0:T(8,128)S(1)} custom-call(s32[2]{0:T(128)S(1)} %add_convert_fusion.4.flags, bf16[96,8192]{1,0:T(8,128)(2,1)S(1)} %collective-permute-done.13.refs_0_, bf16[96,8192]{1,0:T(8,128)(2,1)S(1)} %collective-permute-done.14.refs_1_, bf16[96,8192]{1,0:T(8,128)(2,1)S(1)} %collective-permute-done.15.refs_2_, ...), custom_call_target="tpu_custom_call" | custom-call | flops 4026531840 | bytes 13303808 | tf_op jit(solution)/shard_map/pallas_call | solution.py:131
  187.1 3.7 %collective-permute-done.16.refs_3_ = bf16[96,4096]{1,0:T(8,128)(2,1)S(1)} collective-permute-done((bf16[96,4096]{1,0:T(8,128)(2,1)S(1)}, bf16[96,4096]{1,0:T(8,128)(2,1)S(1)}, u32[]{:S(2)}, u32[]{:S(2)}) %collective-permute-start.16) | collective-permute-done | bytes 786464 | tf_op jit(solution)/shard_map/ppermute | solution.py:176
  190.9 7.7 %shard_map.63 = bf16[480,1024]{1,0:T(8,128)(2,1)S(1)} custom-call(s32[2]{0:T(128)S(1)} %add_convert_fusion.4.flags, bf16[96,8192]{1,0:T(8,128)(2,1)S(1)} %collective-permute-done.13.refs_0_, bf16[96,8192]{1,0:T(8,128)(2,1)S(1)} %collective-permute-done.14.refs_1_, bf16[96,8192]{1,0:T(8,128)(2,1)S(1)} %collective-permute-done.15.refs_2_, ...), custom_call_target="tpu_custom_call" | custom-call | flops 4026531840 | bytes 13303808 | tf_op jit(solution)/shard_map/pallas_call | solution.py:131
  198.8 2.5 collective-permute-done.20
  204.3 2.9 %convolution_convert_fusion = bf16[1536,768]{1,0:T(8,128)(2,1)S(1)} fusion(bf16[1536,1024]{1,0:T(8,128)(2,1)S(1)} %bitcast.66, bf16[1536,1024]{1,0:T(8,128)(2,1)S(1)} %bitcast_dynamic-update-slice_fusion, s32[]{:T(128)S(6)} %select_n.133), kind=kOutput, calls=%fused_computation.1 | convolution fusion | flops 2417098752 | bytes 7077892 | tf_op jit(solution)/shard_map/dot_general | solution.py:23
  207.2 31.3 %all_to_all.15 = bf16[4,4,96,768]{3,2,1,0:T(8,128)(2,1)S(1)} all-to-all(bf16[4,4,96,768]{3,2,1,0:T(8,128)(2,1)S(1)} %bitcast.67), channel_id=1, replica_groups={{0,1,2,3},{4,5,6,7},{8,9,10,11},{12,13,14,15},{16,17,18,19},{20,21,22,2..., dimensions={0} | all-to-all | bytes 4718592 | tf_op jit(solution)/shard_map/all_to_all | solution.py:224
  239.7 3.9 %all-to-all-start.1 = ((bf16[4,96,768]{2,1,0:T(8,128)(2,1)}), bf16[4,96,768]{2,1,0:T(8,128)(2,1)S(1)}, u32[]{:S(2)}, u32[]{:S(2)}) async-start(bf16[4,96,768]{2,1,0:T(8,128)(2,1)} %convert_element_type.66), calls=%async_computation.1 | async-start | bytes 1179648 | tf_op jit(solution)/shard_map/all_to_all | solution.py:227
  243.9 14.7 %all-to-all-done.1 = bf16[4,96,768]{2,1,0:T(8,128)(2,1)S(1)} async-done(((bf16[4,96,768]{2,1,0:T(8,128)(2,1)}), bf16[4,96,768]{2,1,0:T(8,128)(2,1)S(1)}, u32[]{:S(2)}, u32[]{:S(2)}) %all-to-all-start.1) | async-done | bytes 589856 | tf_op jit(solution)/shard_map/all_to_all | solution.py:227
  260.9 9.5 %all_to_all.16 = f32[32,1,128]{2,1,0:T(1,128)S(1)} all-to-all(f32[32,1,128]{2,1,0:T(1,128)S(1)} %broadcast_in_dim.30), channel_id=1, replica_groups=mesh['aux'=2,'pair'=16] {'aux','pair'}, dimensions={0} | all-to-all | bytes 32768 | tf_op jit(solution)/shard_map/all_to_all | solution.py:19
  (72 shorter events, 20.4 us)
Async XLA Ops:
  0.6 93.9 %copy-start = (bf16[8192,96]{0,1:T(8,128)(2,1)S(1)}, bf16[8192,96]{0,1:T(8,128)(2,1)}, u32[]{:S(2)}) copy-start(bf16[8192,96]{0,1:T(8,128)(2,1)} %param.5) | copy-start | bytes 4718596
  0.6 39.0 %collective-permute-start.4 = (bf16[96,8192]{1,0:T(8,128)(2,1)}, bf16[96,8192]{1,0:T(8,128)(2,1)}, u32[]{:S(2)}, u32[]{:S(2)}) collective-permute-start(bf16[96,8192]{1,0:T(8,128)(2,1)} %bitcast.45), channel_id=1, source_target_pairs={{0,4},{1,5},{2,6},{3,7},{4,8},{5,9},{6,10},{7,11},{8,12},{9,13},{1... | collective-permute-start | bytes 4718600 | tf_op jit(solution)/shard_map/ppermute | solution.py:176
  5.7 37.3 %collective-permute-start.1 = (bf16[96,8192]{1,0:T(8,128)(2,1)}, bf16[96,8192]{1,0:T(8,128)(2,1)S(1)}, u32[]{:S(2)}, u32[]{:S(2)}) collective-permute-start(bf16[96,8192]{1,0:T(8,128)(2,1)} %bitcast.46), channel_id=1, source_target_pairs={{0,2},{1,3},{2,0},{3,1},{4,6},{5,7},{6,4},{7,5},{8,10},{9,11},{10,... | collective-permute-start | bytes 4718600 | tf_op jit(solution)/shard_map/ppermute | solution.py:167
  9.2 35.1 %collective-permute-start = (bf16[96,8192]{1,0:T(8,128)(2,1)}, bf16[96,8192]{1,0:T(8,128)(2,1)}, u32[]{:S(2)}, u32[]{:S(2)}) collective-permute-start(bf16[96,8192]{1,0:T(8,128)(2,1)} %bitcast.47), channel_id=1, source_target_pairs={{0,1},{1,0},{2,3},{3,2},{4,5},{5,4},{6,7},{7,6},{8,9},{9,8},{10,11... | collective-permute-start | bytes 4718600 | tf_op jit(solution)/shard_map/ppermute | solution.py:167
  39.7 22.6 %collective-permute-start.5 = (bf16[96,8192]{1,0:T(8,128)(2,1)}, bf16[96,8192]{1,0:T(8,128)(2,1)}, u32[]{:S(2)}, u32[]{:S(2)}) collective-permute-start(bf16[96,8192]{1,0:T(8,128)(2,1)} %collective-permute-done.4.refs_0_), channel_id=1, source_target_pairs={{0,1},{1,0},{2,3},{3,2},{4,5},{5,4},{6,7},{7,6},{8,9},{9,8},{10,11... | collective-permute-start | bytes 4718600 | tf_op jit(solution)/shard_map/ppermute | solution.py:167
  43.1 1.2 copy-start.1
  44.3 25.0 %collective-permute-start.9 = (bf16[96,8192]{1,0:T(8,128)(2,1)}, bf16[96,8192]{1,0:T(8,128)(2,1)S(1)}, u32[]{:S(2)}, u32[]{:S(2)}) collective-permute-start(bf16[96,8192]{1,0:T(8,128)(2,1)} %collective-permute-done.4.refs_0_), channel_id=1, source_target_pairs={{0,4},{1,5},{2,6},{3,7},{4,8},{5,9},{6,10},{7,11},{8,12},{9,13},{1... | collective-permute-start | bytes 4718600 | tf_op jit(solution)/shard_map/ppermute | solution.py:176
  48.7 22.6 %collective-permute-start.2 = (bf16[96,8192]{1,0:T(8,128)(2,1)}, bf16[96,8192]{1,0:T(8,128)(2,1)}, u32[]{:S(2)}, u32[]{:S(2)}) collective-permute-start(bf16[96,8192]{1,0:T(8,128)(2,1)} %collective-permute-done.refs_1_), channel_id=1, source_target_pairs={{0,2},{1,3},{2,0},{3,1},{4,6},{5,7},{6,4},{7,5},{8,10},{9,11},{10,... | collective-permute-start | bytes 4718600 | tf_op jit(solution)/shard_map/ppermute | solution.py:167
  52.1 42.4 %copy-start.2 = (bf16[96,8192]{1,0:T(8,128)(2,1)S(1)}, bf16[96,8192]{1,0:T(8,128)(2,1)}, u32[]{:S(2)}) copy-start(bf16[96,8192]{1,0:T(8,128)(2,1)} %copy-done.1) | copy-start | bytes 4718596
  52.2 54.0 %collective-permute-start.6 = (bf16[96,8192]{1,0:T(8,128)(2,1)}, bf16[96,8192]{1,0:T(8,128)(2,1)S(1)}, u32[]{:S(2)}, u32[]{:S(2)}) collective-permute-start(bf16[96,8192]{1,0:T(8,128)(2,1)} %collective-permute-done.4.refs_0_), channel_id=1, source_target_pairs={{0,2},{1,3},{2,0},{3,1},{4,6},{5,7},{6,4},{7,5},{8,10},{9,11},{10,... | collective-permute-start | bytes 4718600 | tf_op jit(solution)/shard_map/ppermute | solution.py:167
  62.3 52.1 %collective-permute-start.7 = (bf16[96,8192]{1,0:T(8,128)(2,1)}, bf16[96,8192]{1,0:T(8,128)(2,1)S(1)}, u32[]{:S(2)}, u32[]{:S(2)}) collective-permute-start(bf16[96,8192]{1,0:T(8,128)(2,1)} %collective-permute-done.5.refs_1_), channel_id=1, source_target_pairs={{0,2},{1,3},{2,0},{3,1},{4,6},{5,7},{6,4},{7,5},{8,10},{9,11},{10,... | collective-permute-start | bytes 4718600 | tf_op jit(solution)/shard_map/ppermute | solution.py:167
  71.3 34.8 %collective-permute-start.10 = (bf16[96,8192]{1,0:T(8,128)(2,1)S(1)}, bf16[96,8192]{1,0:T(8,128)(2,1)S(1)}, u32[]{:S(2)}, u32[]{:S(2)}) collective-permute-start(bf16[96,8192]{1,0:T(8,128)(2,1)S(1)} %collective-permute-done.9.refs_0_), channel_id=1, source_target_pairs={{0,1},{1,0},{2,3},{3,2},{4,5},{5,4},{6,7},{7,6},{8,9},{9,8},{10,11... | collective-permute-start | bytes 4718600 | tf_op jit(solution)/shard_map/ppermute | solution.py:167
  75.3 52.0 %collective-permute-start.14 = (bf16[96,8192]{1,0:T(8,128)(2,1)S(1)}, bf16[96,8192]{1,0:T(8,128)(2,1)S(1)}, u32[]{:S(2)}, u32[]{:S(2)}) collective-permute-start(bf16[96,8192]{1,0:T(8,128)(2,1)S(1)} %broadcast_select_fusion.1), channel_id=1, source_target_pairs={{0,4},{1,5},{2,6},{3,7},{4,8},{5,9},{6,10},{7,11},{8,12},{9,13},{1... | collective-permute-start | bytes 4718600 | tf_op jit(solution)/shard_map/ppermute | solution.py:176
  91.1 38.7 %collective-permute-start.11 = (bf16[96,8192]{1,0:T(8,128)(2,1)S(1)}, bf16[96,8192]{1,0:T(8,128)(2,1)S(1)}, u32[]{:S(2)}, u32[]{:S(2)}) collective-permute-start(bf16[96,8192]{1,0:T(8,128)(2,1)S(1)} %collective-permute-done.9.refs_0_), channel_id=1, source_target_pairs={{0,2},{1,3},{2,0},{3,1},{4,6},{5,7},{6,4},{7,5},{8,10},{9,11},{10,... | collective-permute-start | bytes 4718600 | tf_op jit(solution)/shard_map/ppermute | solution.py:167
  106.1 2.7 %collective-permute-start.3 = (bf16[384,1024]{1,0:T(8,128)(2,1)S(1)}, bf16[384,1024]{1,0:T(8,128)(2,1)S(1)}, u32[]{:S(2)}, u32[]{:S(2)}) collective-permute-start(bf16[384,1024]{1,0:T(8,128)(2,1)S(1)} %shard_map.59), channel_id=1, source_target_pairs={{0,16},{16,0},{1,17},{17,1},{2,18},{18,2},{3,19},{19,3},{4,20},{20... | collective-permute-start | bytes 2359304 | tf_op jit(solution)/shard_map/ppermute | solution.py:182
  106.2 33.3 %collective-permute-start.13 = (bf16[96,8192]{1,0:T(8,128)(2,1)S(1)}, bf16[96,8192]{1,0:T(8,128)(2,1)S(1)}, u32[]{:S(2)}, u32[]{:S(2)}) collective-permute-start(bf16[96,8192]{1,0:T(8,128)(2,1)S(1)} %collective-permute-done.10.refs_1_), channel_id=1, source_target_pairs={{0,2},{1,3},{2,0},{3,1},{4,6},{5,7},{6,4},{7,5},{8,10},{9,11},{10,... | collective-permute-start | bytes 4718600 | tf_op jit(solution)/shard_map/ppermute | solution.py:167
  108.9 55.8 %collective-permute-start.15 = (bf16[96,8192]{1,0:T(8,128)(2,1)S(1)}, bf16[96,8192]{1,0:T(8,128)(2,1)S(1)}, u32[]{:S(2)}, u32[]{:S(2)}) collective-permute-start(bf16[96,8192]{1,0:T(8,128)(2,1)S(1)} %broadcast_select_fusion), channel_id=1, source_target_pairs={{0,4},{1,5},{2,6},{3,7},{4,8},{5,9},{6,10},{7,11},{8,12},{9,13},{1... | collective-permute-start | bytes 4718600 | tf_op jit(solution)/shard_map/ppermute | solution.py:176
  126.0 47.1 %collective-permute-start.8 = (bf16[384,1024]{1,0:T(8,128)(2,1)S(1)}, bf16[384,1024]{1,0:T(8,128)(2,1)S(1)}, u32[]{:S(2)}, u32[]{:S(2)}) collective-permute-start(bf16[384,1024]{1,0:T(8,128)(2,1)S(1)} %shard_map.60), channel_id=1, source_target_pairs={{0,16},{16,0},{1,17},{17,1},{2,18},{18,2},{3,19},{19,3},{4,20},{20... | collective-permute-start | bytes 2359304 | tf_op jit(solution)/shard_map/ppermute | solution.py:182
  127.4 51.3 %collective-permute-start.18 = (bf16[96,4096]{1,0:T(8,128)(2,1)S(1)}, bf16[96,4096]{1,0:T(8,128)(2,1)S(1)}, u32[]{:S(2)}, u32[]{:S(2)}) collective-permute-start(bf16[96,4096]{1,0:T(8,128)(2,1)S(1)} %slice.22), channel_id=1, source_target_pairs={{0,2},{1,3},{2,0},{3,1},{4,6},{5,7},{6,4},{7,5},{8,10},{9,11},{10,... | collective-permute-start | bytes 2359304 | tf_op jit(solution)/shard_map/ppermute | solution.py:167
  139.5 29.3 %collective-permute-start.12 = (bf16[288,1024]{1,0:T(8,128)(2,1)S(1)}, bf16[288,1024]{1,0:T(8,128)(2,1)S(1)}, u32[]{:S(2)}, u32[]{:S(2)}) collective-permute-start(bf16[288,1024]{1,0:T(8,128)(2,1)S(1)} %shard_map.61), channel_id=1, source_target_pairs={{0,16},{16,0},{1,17},{17,1},{2,18},{18,2},{3,19},{19,3},{4,20},{20... | collective-permute-start | bytes 1769480 | tf_op jit(solution)/shard_map/ppermute | solution.py:182
  164.8 13.9 %collective-permute-start.19 = (bf16[96,4096]{1,0:T(8,128)(2,1)S(1)}, bf16[96,4096]{1,0:T(8,128)(2,1)S(1)}, u32[]{:S(2)}, u32[]{:S(2)}) collective-permute-start(bf16[96,4096]{1,0:T(8,128)(2,1)S(1)} %get-tuple-element.29), channel_id=1, source_target_pairs={{0,2},{1,3},{2,0},{3,1},{4,6},{5,7},{6,4},{7,5},{8,10},{9,11},{10,... | collective-permute-start | bytes 2359304 | tf_op jit(solution)/shard_map/ppermute | solution.py:167
  166.9 24.0 %collective-permute-start.16 = (bf16[96,4096]{1,0:T(8,128)(2,1)S(1)}, bf16[96,4096]{1,0:T(8,128)(2,1)S(1)}, u32[]{:S(2)}, u32[]{:S(2)}) collective-permute-start(bf16[96,4096]{1,0:T(8,128)(2,1)S(1)} %slice_select_fusion), channel_id=1, source_target_pairs={{0,4},{1,5},{2,6},{3,7},{4,8},{5,9},{6,10},{7,11},{8,12},{9,13},{1... | collective-permute-start | bytes 2359304 | tf_op jit(solution)/shard_map/ppermute | solution.py:176
  168.8 18.4 %collective-permute-start.17 = (bf16[96,4096]{1,0:T(8,128)(2,1)S(1)}, bf16[96,4096]{1,0:T(8,128)(2,1)S(1)}, u32[]{:S(2)}, u32[]{:S(2)}) collective-permute-start(bf16[96,4096]{1,0:T(8,128)(2,1)S(1)} %get-tuple-element.27), channel_id=1, source_target_pairs={{0,2},{1,3},{2,0},{3,1},{4,6},{5,7},{6,4},{7,5},{8,10},{9,11},{10,... | collective-permute-start | bytes 2359304 | tf_op jit(solution)/shard_map/ppermute | solution.py:167
  198.6 4.3 %copy-start.3 = (bf16[384,1024]{1,0:T(8,128)(2,1)S(1)}, bf16[384,1024]{1,0:T(8,128)(2,1)}, u32[]{:S(2)}) copy-start(bf16[384,1024]{1,0:T(8,128)(2,1)} %add_convert_fusion.2) | copy-start | bytes 2359300
  198.6 2.8 %collective-permute-start.20 = (bf16[480,1024]{1,0:T(8,128)(2,1)S(1)}, bf16[480,1024]{1,0:T(8,128)(2,1)}, u32[]{:S(2)}, u32[]{:S(2)}) collective-permute-start(bf16[480,1024]{1,0:T(8,128)(2,1)S(1)} %shard_map.63), channel_id=1, source_target_pairs={{0,16},{16,0},{1,17},{17,1},{2,18},{18,2},{3,19},{19,3},{4,20},{20... | collective-permute-start | bytes 2949128 | tf_op jit(solution)/shard_map/ppermute | solution.py:182
  238.5 5.2 %copy-start.4 = (f32[768]{0:T(1024)S(1)}, f32[768]{0:T(1024)}, u32[]{:S(2)}) copy-start(f32[768]{0:T(1024)} %param.7) | copy-start | bytes 9220
  238.5 5.2 %copy-start.5 = (f32[2]{0:T(128)S(1)}, f32[2]{0:T(128)}, u32[]{:S(2)}) copy-start(f32[2]{0:T(128)} %param.6) | copy-start | bytes 28
  239.7 18.9 %all-to-all-start.1 = ((bf16[4,96,768]{2,1,0:T(8,128)(2,1)}), bf16[4,96,768]{2,1,0:T(8,128)(2,1)S(1)}, u32[]{:S(2)}, u32[]{:S(2)}) async-start(bf16[4,96,768]{2,1,0:T(8,128)(2,1)} %convert_element_type.66), calls=%async_computation.1 | async-start | bytes 1179648 | tf_op jit(solution)/shard_map/all_to_all | solution.py:227

commit v2 on v1

--- a/solution.py
+++ b/solution.py
@@ -207,22 +207,35 @@
     fitted_3 = fitted_of([plane_2[3], above_3, near_3, far_3[1], both_3[1]], 1, 2, partial_3)[1]
     fitted = jnp.concatenate([fitted_0, fitted_1, fitted_2, fitted_3])
     blocks = fitted.reshape(pair_count, share_rows, rows)
-    ordered = []
-    for z in range(LAYERS):
-        slot = (layer - z) % LAYERS
-        for where in range(PLANE):
-            offset = place ^ where
-            at = slot * PLANE + offset
-            ordered.append(lax.dynamic_index_in_dim(blocks, at, 0, keepdims=False))
-    fitted = jnp.concatenate(ordered)
-    own_share = lax.dynamic_slice_in_dim(fitted, aux_id * share_cols, share_cols, 0)
-    grid = (LAYERS, PLANE, share_rows, rows)
-    turned = jnp.swapaxes(fitted.reshape(grid), 0, 1).reshape(fitted.shape)
-    partial_tiles = nt_dot(turned, own_share).astype(jnp.bfloat16)
-    tiles = partial_tiles.reshape(PLANE, LAYERS, share_rows, share_cols)
+
+    def block_of(z, offset):
+        at = (layer - z) % LAYERS * PLANE + offset
+        return lax.dynamic_index_in_dim(blocks, at, 0, keepdims=False)
+
+    own_layers = LAYERS // 2
+    own_share = jnp.concatenate(
+        [
+            block_of(aux_id * own_layers + z, place ^ where)
+            for z in range(own_layers)
+            for where in range(PLANE)
+        ]
+    )
+    turn = [jnp.where(aux_id == 0, bits[0], bits[1]) for bits in (TURN, TURN[::-1])]
+
+    def tiles_for(offsets):
+        left = jnp.concatenate([block_of(z, offset) for offset in offsets for z in range(LAYERS)])
+        return nt_dot(left, own_share).reshape(2, LAYERS, share_rows, share_cols)
+
+    def everywhere(bits):
+        count = LAYERS * PLANE
+        return [(core * count + i, core * count + (i ^ bits[core])) for core in range(2) for i in range(count)]
+
+    sent = tiles_for([turn[0], 3]).astype(jnp.bfloat16)
+    came = lax.ppermute(sent, AXES, everywhere(TURN))
+    kept = tiles_for([0, turn[1]]) + came.astype(jnp.float32)
+    came = lax.ppermute(kept[1].astype(jnp.bfloat16), AXES, everywhere(TURN[::-1]))
+    sums = kept[0] + came.astype(jnp.float32)
     chips = [list(range(z * PLANE, (z + 1) * PLANE)) for z in range(LAYERS)]
-    tiles = lax.all_to_all(tiles, "pair", 0, 0, tiled=True, axis_index_groups=chips)
-    sums = jnp.sum(tiles.astype(jnp.float32), axis=0)
     columns = [list(group) for group in zip(*chips)]
     tiles = lax.all_to_all(
         sums.astype(jnp.bfloat16), "pair", 0, 0, tiled=True, axis_index_groups=columns

time: 274 us -> 267 us (0.974)
  blocking collectives: 40.7 us -> 10 us
  waiting for transfers between devices: 93.4 us -> 117 us
    all_to_all x1 -> x0, blocking collectives: 31.3 us -> none  [shards_stacked(): lax.all_to_all(tiles, 'pair', 0, 0, tiled=True, axis_index_groups=chips)]
    ppermute x0 -> x2, waiting for transfers between devices: none -> 22.3 us  [the longest x1 14.1 us: shards_stacked(): came = lax.ppermute(sent, AXES, everywhere(TURN))]
  transfers between devices with their start and end apart: 22 -> 24, of which waited for: 11 -> 13; matrix products, arithmetic and copies ran while one was open for 2% -> 2% of each run, Pallas kernels for 15% -> 15%
where the time goes in v2:
time: 267 us; the launch traced here: 266 us
  waiting for transfers between devices  117 us (44%)
  starting transfers between devices  74.1 us (28%)
  Pallas kernels  47.9 us (18%)
  blocking collectives  10 us (4%)
  other arithmetic  8.34 us (3%)
  between operations  3.25 us (1%)
  matrix products  2.85 us (1%)
  local copies, waits for them, and re-layouts  2.68 us (1%)
    ppermute x5, waiting for transfers between devices, climb(): return lax.ppermute(tied(piece, after), AXES, climbs(stage))  62.2 us
    pallas_call x5, Pallas kernels, fit(): pl.pallas_call(functools.partial(fit_kernel, len(pieces)), out_shape=jax....  47.9 us
    ppermute x12, starting transfers between devices, cross(): crossed.append(lax.ppermute(tied(piece, after), AXES, along(turn)))  36.4 us
    ppermute x5, starting transfers between devices, climb(): return lax.ppermute(tied(piece, after), AXES, climbs(stage))  31.4 us
    ppermute x12, waiting for transfers between devices, cross(): crossed.append(lax.ppermute(tied(piece, after), AXES, along(turn)))  15.2 us
    all_to_all x1, waiting for transfers between devices, shards_stacked(): lax.all_to_all(sums.astype(jnp.bfloat16), 'pair', 0, 0, tiled=True, axis_...  14.4 us
    ppermute x1, waiting for transfers between devices, shards_stacked(): came = lax.ppermute(sent, AXES, everywhere(TURN))  14.1 us
    all_to_all x1, blocking collectives, total_of(): return jnp.sum(lax.all_to_all(sent, axes, 0, 0, tiled=True)[:, 0, 0])  10 us
  transfers between devices with their start and end apart: 24, of which 13 were waited for; matrix products, arithmetic and copies ran while one was open for 2% of the time, Pallas kernels for 15%

profile of v2, /device:TPU:0, one launch (start us, length us, event | category | flops | bytes accessed | tf_op | source)
XLA Modules:
  0.0 265.7 jit_solution(18090423340937740270)
XLA Ops:
  0.6 4.9 %collective-permute-start.4 = (bf16[96,8192]{1,0:T(8,128)(2,1)}, bf16[96,8192]{1,0:T(8,128)(2,1)}, u32[]{:S(2)}, u32[]{:S(2)}) collective-permute-start(bf16[96,8192]{1,0:T(8,128)(2,1)} %bitcast.68), channel_id=1, source_target_pairs={{0,4},{1,5},{2,6},{3,7},{4,8},{5,9},{6,10},{7,11},{8,12},{9,13},{1... | collective-permute-start | bytes 4718600 | tf_op jit(solution)/shard_map/ppermute | solution.py:176
  5.6 3.4 %collective-permute-start.1 = (bf16[96,8192]{1,0:T(8,128)(2,1)}, bf16[96,8192]{1,0:T(8,128)(2,1)S(1)}, u32[]{:S(2)}, u32[]{:S(2)}) collective-permute-start(bf16[96,8192]{1,0:T(8,128)(2,1)} %bitcast.69), channel_id=1, source_target_pairs={{0,2},{1,3},{2,0},{3,1},{4,6},{5,7},{6,4},{7,5},{8,10},{9,11},{10,... | collective-permute-start | bytes 4718600 | tf_op jit(solution)/shard_map/ppermute | solution.py:167
  9.0 3.4 %collective-permute-start = (bf16[96,8192]{1,0:T(8,128)(2,1)}, bf16[96,8192]{1,0:T(8,128)(2,1)S(1)}, u32[]{:S(2)}, u32[]{:S(2)}) collective-permute-start(bf16[96,8192]{1,0:T(8,128)(2,1)} %bitcast.70), channel_id=1, source_target_pairs={{0,1},{1,0},{2,3},{3,2},{4,5},{5,4},{6,7},{7,6},{8,9},{9,8},{10,11... | collective-permute-start | bytes 4718600 | tf_op jit(solution)/shard_map/ppermute | solution.py:167
  12.4 27.1 %collective-permute-done.4.refs_0_ = bf16[96,8192]{1,0:T(8,128)(2,1)} collective-permute-done((bf16[96,8192]{1,0:T(8,128)(2,1)}, bf16[96,8192]{1,0:T(8,128)(2,1)}, u32[]{:S(2)}, u32[]{:S(2)}) %collective-permute-start.4) | collective-permute-done | bytes 1572896 | tf_op jit(solution)/shard_map/ppermute | solution.py:176
  39.5 3.4 %collective-permute-start.5 = (bf16[96,8192]{1,0:T(8,128)(2,1)}, bf16[96,8192]{1,0:T(8,128)(2,1)}, u32[]{:S(2)}, u32[]{:S(2)}) collective-permute-start(bf16[96,8192]{1,0:T(8,128)(2,1)} %collective-permute-done.4.refs_0_), channel_id=1, source_target_pairs={{0,1},{1,0},{2,3},{3,2},{4,5},{5,4},{6,7},{7,6},{8,9},{9,8},{10,11... | collective-permute-start | bytes 4718600 | tf_op jit(solution)/shard_map/ppermute | solution.py:167
  44.1 4.4 %collective-permute-start.9 = (bf16[96,8192]{1,0:T(8,128)(2,1)}, bf16[96,8192]{1,0:T(8,128)(2,1)S(1)}, u32[]{:S(2)}, u32[]{:S(2)}) collective-permute-start(bf16[96,8192]{1,0:T(8,128)(2,1)} %collective-permute-done.4.refs_0_), channel_id=1, source_target_pairs={{0,4},{1,5},{2,6},{3,7},{4,8},{5,9},{6,10},{7,11},{8,12},{9,13},{1... | collective-permute-start | bytes 4718600 | tf_op jit(solution)/shard_map/ppermute | solution.py:176
  48.5 3.4 %collective-permute-start.2 = (bf16[96,8192]{1,0:T(8,128)(2,1)S(1)}, bf16[96,8192]{1,0:T(8,128)(2,1)}, u32[]{:S(2)}, u32[]{:S(2)}) collective-permute-start(bf16[96,8192]{1,0:T(8,128)(2,1)S(1)} %collective-permute-done.refs_1_), channel_id=1, source_target_pairs={{0,2},{1,3},{2,0},{3,1},{4,6},{5,7},{6,4},{7,5},{8,10},{9,11},{10,... | collective-permute-start | bytes 4718600 | tf_op jit(solution)/shard_map/ppermute | solution.py:167
  52.0 2.7 %collective-permute-start.6 = (bf16[96,8192]{1,0:T(8,128)(2,1)}, bf16[96,8192]{1,0:T(8,128)(2,1)S(1)}, u32[]{:S(2)}, u32[]{:S(2)}) collective-permute-start(bf16[96,8192]{1,0:T(8,128)(2,1)} %collective-permute-done.4.refs_0_), channel_id=1, source_target_pairs={{0,2},{1,3},{2,0},{3,1},{4,6},{5,7},{6,4},{7,5},{8,10},{9,11},{10,... | collective-permute-start | bytes 4718600 | tf_op jit(solution)/shard_map/ppermute | solution.py:167
  54.7 7.4 %collective-permute-done.5.refs_1_ = bf16[96,8192]{1,0:T(8,128)(2,1)} collective-permute-done((bf16[96,8192]{1,0:T(8,128)(2,1)}, bf16[96,8192]{1,0:T(8,128)(2,1)}, u32[]{:S(2)}, u32[]{:S(2)}) %collective-permute-start.5) | collective-permute-done | bytes 1572896 | tf_op jit(solution)/shard_map/ppermute | solution.py:167
  62.1 3.4 %collective-permute-start.7 = (bf16[96,8192]{1,0:T(8,128)(2,1)}, bf16[96,8192]{1,0:T(8,128)(2,1)S(1)}, u32[]{:S(2)}, u32[]{:S(2)}) collective-permute-start(bf16[96,8192]{1,0:T(8,128)(2,1)} %collective-permute-done.5.refs_1_), channel_id=1, source_target_pairs={{0,2},{1,3},{2,0},{3,1},{4,6},{5,7},{6,4},{7,5},{8,10},{9,11},{10,... | collective-permute-start | bytes 4718600 | tf_op jit(solution)/shard_map/ppermute | solution.py:167
  65.6 3.5 %collective-permute-done.9.refs_0_ = bf16[96,8192]{1,0:T(8,128)(2,1)S(1)} collective-permute-done((bf16[96,8192]{1,0:T(8,128)(2,1)}, bf16[96,8192]{1,0:T(8,128)(2,1)S(1)}, u32[]{:S(2)}, u32[]{:S(2)}) %collective-permute-start.9) | collective-permute-done | bytes 1572896 | tf_op jit(solution)/shard_map/ppermute | solution.py:176
  70.9 2.4 collective-permute-start.10
  74.9 15.9 %collective-permute-start.14 = (bf16[96,8192]{1,0:T(8,128)(2,1)S(1)}, bf16[96,8192]{1,0:T(8,128)(2,1)S(1)}, u32[]{:S(2)}, u32[]{:S(2)}) collective-permute-start(bf16[96,8192]{1,0:T(8,128)(2,1)S(1)} %broadcast_select_fusion.1), channel_id=1, source_target_pairs={{0,4},{1,5},{2,6},{3,7},{4,8},{5,9},{6,10},{7,11},{8,12},{9,13},{1... | collective-permute-start | bytes 4718600 | tf_op jit(solution)/shard_map/ppermute | solution.py:176
  90.8 3.4 %collective-permute-start.11 = (bf16[96,8192]{1,0:T(8,128)(2,1)S(1)}, bf16[96,8192]{1,0:T(8,128)(2,1)S(1)}, u32[]{:S(2)}, u32[]{:S(2)}) collective-permute-start(bf16[96,8192]{1,0:T(8,128)(2,1)S(1)} %collective-permute-done.9.refs_0_), channel_id=1, source_target_pairs={{0,2},{1,3},{2,0},{3,1},{4,6},{5,7},{6,4},{7,5},{8,10},{9,11},{10,... | collective-permute-start | bytes 4718600 | tf_op jit(solution)/shard_map/ppermute | solution.py:167
  94.3 11.1 %shard_map.59 = bf16[384,1024]{1,0:T(8,128)(2,1)S(1)} custom-call(s32[2]{0:T(128)S(1)} %add_convert_fusion.4.flags, bf16[96,8192]{1,0:T(8,128)(2,1)S(1)} %bitcast.71, bf16[96,8192]{1,0:T(8,128)(2,1)S(1)} %collective-permute-done.refs_1_, bf16[96,8192]{1,0:T(8,128)(2,1)S(1)} %copy-done.2, bf16[96,8192]{1,0:T(8,128)(2,1)} %collective-permute-done.2.refs_3_, ...), custom_call_target="tpu_custom_call" | custom-call | flops 6442450944 | bytes 23855104 | tf_op jit(solution)/shard_map/pallas_call | solution.py:131
  105.5 2.4 collective-permute-start.13
  108.2 4.3 %collective-permute-start.15 = (bf16[96,8192]{1,0:T(8,128)(2,1)S(1)}, bf16[96,8192]{1,0:T(8,128)(2,1)S(1)}, u32[]{:S(2)}, u32[]{:S(2)}) collective-permute-start(bf16[96,8192]{1,0:T(8,128)(2,1)S(1)} %broadcast_select_fusion), channel_id=1, source_target_pairs={{0,4},{1,5},{2,6},{3,7},{4,8},{5,9},{6,10},{7,11},{8,12},{9,13},{1... | collective-permute-start | bytes 4718600 | tf_op jit(solution)/shard_map/ppermute | solution.py:176
  112.8 11.7 %shard_map.60 = bf16[384,1024]{1,0:T(8,128)(2,1)S(1)} custom-call(s32[2]{0:T(128)S(1)} %add_convert_fusion.4.flags, bf16[96,8192]{1,0:T(8,128)(2,1)} %collective-permute-done.4.refs_0_, bf16[96,8192]{1,0:T(8,128)(2,1)} %collective-permute-done.5.refs_1_, bf16[96,8192]{1,0:T(8,128)(2,1)S(1)} %collective-permute-done.6.refs_2_, ...), custom_call_target="tpu_custom_call" | custom-call | flops 6442450944 | bytes 23855104 | tf_op jit(solution)/shard_map/pallas_call | solution.py:131
  124.5 2.5 collective-permute-done.14.refs_1_
  127.0 2.4 collective-permute-start.18
  129.5 9.7 %shard_map.61 = bf16[288,1024]{1,0:T(8,128)(2,1)S(1)} custom-call(s32[2]{0:T(128)S(1)} %add_convert_fusion.4.flags, bf16[96,8192]{1,0:T(8,128)(2,1)S(1)} %collective-permute-done.9.refs_0_, bf16[96,8192]{1,0:T(8,128)(2,1)S(1)} %collective-permute-done.10.refs_1_, bf16[96,8192]{1,0:T(8,128)(2,1)S(1)} %collective-permute-done.11.refs_2_, ...), custom_call_target="tpu_custom_call" | custom-call | flops 4831838208 | bytes 22085632 | tf_op jit(solution)/shard_map/pallas_call | solution.py:131
  139.2 25.3 %collective-permute-done.15.refs_2_ = bf16[96,8192]{1,0:T(8,128)(2,1)S(1)} collective-permute-done((bf16[96,8192]{1,0:T(8,128)(2,1)S(1)}, bf16[96,8192]{1,0:T(8,128)(2,1)S(1)}, u32[]{:S(2)}, u32[]{:S(2)}) %collective-permute-start.15) | collective-permute-done | bytes 1572896 | tf_op jit(solution)/shard_map/ppermute | solution.py:176
  168.7 4.1 %collective-permute-start.17 = (bf16[96,4096]{1,0:T(8,128)(2,1)S(1)}, bf16[96,4096]{1,0:T(8,128)(2,1)S(1)}, u32[]{:S(2)}, u32[]{:S(2)}) collective-permute-start(bf16[96,4096]{1,0:T(8,128)(2,1)S(1)} %get-tuple-element.27), channel_id=1, source_target_pairs={{0,2},{1,3},{2,0},{3,1},{4,6},{5,7},{6,4},{7,5},{8,10},{9,11},{10,... | collective-permute-start | bytes 2359304 | tf_op jit(solution)/shard_map/ppermute | solution.py:167
  173.3 5.3 %collective-permute-done.19.refs_4_ = bf16[96,4096]{1,0:T(8,128)(2,1)S(1)} collective-permute-done((bf16[96,4096]{1,0:T(8,128)(2,1)S(1)}, bf16[96,4096]{1,0:T(8,128)(2,1)S(1)}, u32[]{:S(2)}, u32[]{:S(2)}) %collective-permute-start.19) | collective-permute-done | bytes 786464 | tf_op jit(solution)/shard_map/ppermute | solution.py:167
  178.6 7.7 %shard_map.62.refs_6_ = f32[480,1024]{1,0:T(8,128)S(1)} custom-call(s32[2]{0:T(128)S(1)} %add_convert_fusion.4.flags, bf16[96,8192]{1,0:T(8,128)(2,1)S(1)} %collective-permute-done.13.refs_0_, bf16[96,8192]{1,0:T(8,128)(2,1)S(1)} %collective-permute-done.14.refs_1_, bf16[96,8192]{1,0:T(8,128)(2,1)S(1)} %collective-permute-done.15.refs_2_, ...), custom_call_target="tpu_custom_call" | custom-call | flops 4026531840 | bytes 13303808 | tf_op jit(solution)/shard_map/pallas_call | solution.py:131
  187.0 3.8 %collective-permute-done.16.refs_3_ = bf16[96,4096]{1,0:T(8,128)(2,1)S(1)} collective-permute-done((bf16[96,4096]{1,0:T(8,128)(2,1)S(1)}, bf16[96,4096]{1,0:T(8,128)(2,1)S(1)}, u32[]{:S(2)}, u32[]{:S(2)}) %collective-permute-start.16) | collective-permute-done | bytes 786464 | tf_op jit(solution)/shard_map/ppermute | solution.py:176
  190.8 7.7 %shard_map.63 = bf16[480,1024]{1,0:T(8,128)(2,1)S(1)} custom-call(s32[2]{0:T(128)S(1)} %add_convert_fusion.4.flags, bf16[96,8192]{1,0:T(8,128)(2,1)S(1)} %collective-permute-done.13.refs_0_, bf16[96,8192]{1,0:T(8,128)(2,1)S(1)} %collective-permute-done.14.refs_1_, bf16[96,8192]{1,0:T(8,128)(2,1)S(1)} %collective-permute-done.15.refs_2_, ...), custom_call_target="tpu_custom_call" | custom-call | flops 4026531840 | bytes 13303808 | tf_op jit(solution)/shard_map/pallas_call | solution.py:131
  207.3 14.1 %collective-permute-done.21 = bf16[2,4,96,768]{3,2,1,0:T(8,128)(2,1)S(1)} collective-permute-done((bf16[2,4,96,768]{3,2,1,0:T(8,128)(2,1)S(1)}, bf16[2,4,96,768]{3,2,1,0:T(8,128)(2,1)S(1)}, u32[]{:S(2)}, u32[]{:S(2)}) %collective-permute-start.21) | collective-permute-done | bytes 1179680 | tf_op jit(solution)/shard_map/ppermute | solution.py:234
  223.5 8.2 %collective-permute-done.22 = bf16[4,96,768]{2,1,0:T(8,128)(2,1)S(1)} collective-permute-done((bf16[4,96,768]{2,1,0:T(8,128)(2,1)S(1)}, bf16[4,96,768]{2,1,0:T(8,128)(2,1)S(1)}, u32[]{:S(2)}, u32[]{:S(2)}) %collective-permute-start.22) | collective-permute-done | bytes 589856 | tf_op jit(solution)/shard_map/ppermute | solution.py:236
  232.7 3.5 %all-to-all-start = ((bf16[4,96,768]{2,1,0:T(8,128)(2,1)}), bf16[4,96,768]{2,1,0:T(8,128)(2,1)S(1)}, u32[]{:S(2)}, u32[]{:S(2)}) async-start(bf16[4,96,768]{2,1,0:T(8,128)(2,1)} %get-tuple-element.34), calls=%async_computation | async-start | bytes 1179648 | tf_op jit(solution)/shard_map/all_to_all | solution.py:240
  236.5 14.4 %all-to-all-done = bf16[4,96,768]{2,1,0:T(8,128)(2,1)S(1)} async-done(((bf16[4,96,768]{2,1,0:T(8,128)(2,1)}), bf16[4,96,768]{2,1,0:T(8,128)(2,1)S(1)}, u32[]{:S(2)}, u32[]{:S(2)}) %all-to-all-start) | async-done | bytes 589856 | tf_op jit(solution)/shard_map/all_to_all | solution.py:240
  253.2 10.0 %all_to_all.10 = f32[32,1,128]{2,1,0:T(1,128)S(1)} all-to-all(f32[32,1,128]{2,1,0:T(1,128)S(1)} %broadcast_in_dim.30), channel_id=1, replica_groups=mesh['aux'=2,'pair'=16] {'aux','pair'}, dimensions={0} | all-to-all | bytes 32768 | tf_op jit(solution)/shard_map/all_to_all | solution.py:19
  (66 shorter events, 25.4 us)
Async XLA Ops:
  0.6 38.9 %collective-permute-start.4 = (bf16[96,8192]{1,0:T(8,128)(2,1)}, bf16[96,8192]{1,0:T(8,128)(2,1)}, u32[]{:S(2)}, u32[]{:S(2)}) collective-permute-start(bf16[96,8192]{1,0:T(8,128)(2,1)} %bitcast.68), channel_id=1, source_target_pairs={{0,4},{1,5},{2,6},{3,7},{4,8},{5,9},{6,10},{7,11},{8,12},{9,13},{1... | collective-permute-start | bytes 4718600 | tf_op jit(solution)/shard_map/ppermute | solution.py:176
  5.6 37.3 %collective-permute-start.1 = (bf16[96,8192]{1,0:T(8,128)(2,1)}, bf16[96,8192]{1,0:T(8,128)(2,1)S(1)}, u32[]{:S(2)}, u32[]{:S(2)}) collective-permute-start(bf16[96,8192]{1,0:T(8,128)(2,1)} %bitcast.69), channel_id=1, source_target_pairs={{0,2},{1,3},{2,0},{3,1},{4,6},{5,7},{6,4},{7,5},{8,10},{9,11},{10,... | collective-permute-start | bytes 4718600 | tf_op jit(solution)/shard_map/ppermute | solution.py:167
  9.0 35.1 %collective-permute-start = (bf16[96,8192]{1,0:T(8,128)(2,1)}, bf16[96,8192]{1,0:T(8,128)(2,1)S(1)}, u32[]{:S(2)}, u32[]{:S(2)}) collective-permute-start(bf16[96,8192]{1,0:T(8,128)(2,1)} %bitcast.70), channel_id=1, source_target_pairs={{0,1},{1,0},{2,3},{3,2},{4,5},{5,4},{6,7},{7,6},{8,9},{9,8},{10,11... | collective-permute-start | bytes 4718600 | tf_op jit(solution)/shard_map/ppermute | solution.py:167
  39.5 22.6 %collective-permute-start.5 = (bf16[96,8192]{1,0:T(8,128)(2,1)}, bf16[96,8192]{1,0:T(8,128)(2,1)}, u32[]{:S(2)}, u32[]{:S(2)}) collective-permute-start(bf16[96,8192]{1,0:T(8,128)(2,1)} %collective-permute-done.4.refs_0_), channel_id=1, source_target_pairs={{0,1},{1,0},{2,3},{3,2},{4,5},{5,4},{6,7},{7,6},{8,9},{9,8},{10,11... | collective-permute-start | bytes 4718600 | tf_op jit(solution)/shard_map/ppermute | solution.py:167
  42.9 1.2 copy-start.1
  44.1 25.0 %collective-permute-start.9 = (bf16[96,8192]{1,0:T(8,128)(2,1)}, bf16[96,8192]{1,0:T(8,128)(2,1)S(1)}, u32[]{:S(2)}, u32[]{:S(2)}) collective-permute-start(bf16[96,8192]{1,0:T(8,128)(2,1)} %collective-permute-done.4.refs_0_), channel_id=1, source_target_pairs={{0,4},{1,5},{2,6},{3,7},{4,8},{5,9},{6,10},{7,11},{8,12},{9,13},{1... | collective-permute-start | bytes 4718600 | tf_op jit(solution)/shard_map/ppermute | solution.py:176
  48.5 22.4 %collective-permute-start.2 = (bf16[96,8192]{1,0:T(8,128)(2,1)S(1)}, bf16[96,8192]{1,0:T(8,128)(2,1)}, u32[]{:S(2)}, u32[]{:S(2)}) collective-permute-start(bf16[96,8192]{1,0:T(8,128)(2,1)S(1)} %collective-permute-done.refs_1_), channel_id=1, source_target_pairs={{0,2},{1,3},{2,0},{3,1},{4,6},{5,7},{6,4},{7,5},{8,10},{9,11},{10,... | collective-permute-start | bytes 4718600 | tf_op jit(solution)/shard_map/ppermute | solution.py:167
  52.0 42.2 %copy-start = (bf16[8192,96]{0,1:T(8,128)(2,1)S(1)}, bf16[8192,96]{0,1:T(8,128)(2,1)}, u32[]{:S(2)}) copy-start(bf16[8192,96]{0,1:T(8,128)(2,1)} %param.5) | copy-start | bytes 4718596
  52.0 42.3 %copy-start.2 = (bf16[96,8192]{1,0:T(8,128)(2,1)S(1)}, bf16[96,8192]{1,0:T(8,128)(2,1)}, u32[]{:S(2)}) copy-start(bf16[96,8192]{1,0:T(8,128)(2,1)} %copy-done.1) | copy-start | bytes 4718596
  52.0 53.5 %collective-permute-start.6 = (bf16[96,8192]{1,0:T(8,128)(2,1)}, bf16[96,8192]{1,0:T(8,128)(2,1)S(1)}, u32[]{:S(2)}, u32[]{:S(2)}) collective-permute-start(bf16[96,8192]{1,0:T(8,128)(2,1)} %collective-permute-done.4.refs_0_), channel_id=1, source_target_pairs={{0,2},{1,3},{2,0},{3,1},{4,6},{5,7},{6,4},{7,5},{8,10},{9,11},{10,... | collective-permute-start | bytes 4718600 | tf_op jit(solution)/shard_map/ppermute | solution.py:167
  62.1 50.6 %collective-permute-start.7 = (bf16[96,8192]{1,0:T(8,128)(2,1)}, bf16[96,8192]{1,0:T(8,128)(2,1)S(1)}, u32[]{:S(2)}, u32[]{:S(2)}) collective-permute-start(bf16[96,8192]{1,0:T(8,128)(2,1)} %collective-permute-done.5.refs_1_), channel_id=1, source_target_pairs={{0,2},{1,3},{2,0},{3,1},{4,6},{5,7},{6,4},{7,5},{8,10},{9,11},{10,... | collective-permute-start | bytes 4718600 | tf_op jit(solution)/shard_map/ppermute | solution.py:167
  70.9 34.5 %collective-permute-start.10 = (bf16[96,8192]{1,0:T(8,128)(2,1)S(1)}, bf16[96,8192]{1,0:T(8,128)(2,1)S(1)}, u32[]{:S(2)}, u32[]{:S(2)}) collective-permute-start(bf16[96,8192]{1,0:T(8,128)(2,1)S(1)} %collective-permute-done.9.refs_0_), channel_id=1, source_target_pairs={{0,1},{1,0},{2,3},{3,2},{4,5},{5,4},{6,7},{7,6},{8,9},{9,8},{10,11... | collective-permute-start | bytes 4718600 | tf_op jit(solution)/shard_map/ppermute | solution.py:167
  74.9 52.1 %collective-permute-start.14 = (bf16[96,8192]{1,0:T(8,128)(2,1)S(1)}, bf16[96,8192]{1,0:T(8,128)(2,1)S(1)}, u32[]{:S(2)}, u32[]{:S(2)}) collective-permute-start(bf16[96,8192]{1,0:T(8,128)(2,1)S(1)} %broadcast_select_fusion.1), channel_id=1, source_target_pairs={{0,4},{1,5},{2,6},{3,7},{4,8},{5,9},{6,10},{7,11},{8,12},{9,13},{1... | collective-permute-start | bytes 4718600 | tf_op jit(solution)/shard_map/ppermute | solution.py:176
  90.8 38.6 %collective-permute-start.11 = (bf16[96,8192]{1,0:T(8,128)(2,1)S(1)}, bf16[96,8192]{1,0:T(8,128)(2,1)S(1)}, u32[]{:S(2)}, u32[]{:S(2)}) collective-permute-start(bf16[96,8192]{1,0:T(8,128)(2,1)S(1)} %collective-permute-done.9.refs_0_), channel_id=1, source_target_pairs={{0,2},{1,3},{2,0},{3,1},{4,6},{5,7},{6,4},{7,5},{8,10},{9,11},{10,... | collective-permute-start | bytes 4718600 | tf_op jit(solution)/shard_map/ppermute | solution.py:167
  105.4 2.7 %collective-permute-start.3 = (bf16[384,1024]{1,0:T(8,128)(2,1)S(1)}, bf16[384,1024]{1,0:T(8,128)(2,1)S(1)}, u32[]{:S(2)}, u32[]{:S(2)}) collective-permute-start(bf16[384,1024]{1,0:T(8,128)(2,1)S(1)} %shard_map.59), channel_id=1, source_target_pairs={{0,16},{16,0},{1,17},{17,1},{2,18},{18,2},{3,19},{19,3},{4,20},{20... | collective-permute-start | bytes 2359304 | tf_op jit(solution)/shard_map/ppermute | solution.py:182
  105.5 33.7 %collective-permute-start.13 = (bf16[96,8192]{1,0:T(8,128)(2,1)S(1)}, bf16[96,8192]{1,0:T(8,128)(2,1)S(1)}, u32[]{:S(2)}, u32[]{:S(2)}) collective-permute-start(bf16[96,8192]{1,0:T(8,128)(2,1)S(1)} %collective-permute-done.10.refs_1_), channel_id=1, source_target_pairs={{0,2},{1,3},{2,0},{3,1},{4,6},{5,7},{6,4},{7,5},{8,10},{9,11},{10,... | collective-permute-start | bytes 4718600 | tf_op jit(solution)/shard_map/ppermute | solution.py:167
  108.2 56.4 %collective-permute-start.15 = (bf16[96,8192]{1,0:T(8,128)(2,1)S(1)}, bf16[96,8192]{1,0:T(8,128)(2,1)S(1)}, u32[]{:S(2)}, u32[]{:S(2)}) collective-permute-start(bf16[96,8192]{1,0:T(8,128)(2,1)S(1)} %broadcast_select_fusion), channel_id=1, source_target_pairs={{0,4},{1,5},{2,6},{3,7},{4,8},{5,9},{6,10},{7,11},{8,12},{9,13},{1... | collective-permute-start | bytes 4718600 | tf_op jit(solution)/shard_map/ppermute | solution.py:176
  124.5 48.6 %collective-permute-start.8 = (bf16[384,1024]{1,0:T(8,128)(2,1)S(1)}, bf16[384,1024]{1,0:T(8,128)(2,1)S(1)}, u32[]{:S(2)}, u32[]{:S(2)}) collective-permute-start(bf16[384,1024]{1,0:T(8,128)(2,1)S(1)} %shard_map.60), channel_id=1, source_target_pairs={{0,16},{16,0},{1,17},{17,1},{2,18},{18,2},{3,19},{19,3},{4,20},{20... | collective-permute-start | bytes 2359304 | tf_op jit(solution)/shard_map/ppermute | solution.py:182
  127.0 51.6 %collective-permute-start.18 = (bf16[96,4096]{1,0:T(8,128)(2,1)S(1)}, bf16[96,4096]{1,0:T(8,128)(2,1)S(1)}, u32[]{:S(2)}, u32[]{:S(2)}) collective-permute-start(bf16[96,4096]{1,0:T(8,128)(2,1)S(1)} %slice.31), channel_id=1, source_target_pairs={{0,2},{1,3},{2,0},{3,1},{4,6},{5,7},{6,4},{7,5},{8,10},{9,11},{10,... | collective-permute-start | bytes 2359304 | tf_op jit(solution)/shard_map/ppermute | solution.py:167
  139.2 29.5 %collective-permute-start.12 = (bf16[288,1024]{1,0:T(8,128)(2,1)S(1)}, bf16[288,1024]{1,0:T(8,128)(2,1)S(1)}, u32[]{:S(2)}, u32[]{:S(2)}) collective-permute-start(bf16[288,1024]{1,0:T(8,128)(2,1)S(1)} %shard_map.61), channel_id=1, source_target_pairs={{0,16},{16,0},{1,17},{17,1},{2,18},{18,2},{3,19},{19,3},{4,20},{20... | collective-permute-start | bytes 1769480 | tf_op jit(solution)/shard_map/ppermute | solution.py:182
  164.7 13.9 %collective-permute-start.19 = (bf16[96,4096]{1,0:T(8,128)(2,1)S(1)}, bf16[96,4096]{1,0:T(8,128)(2,1)S(1)}, u32[]{:S(2)}, u32[]{:S(2)}) collective-permute-start(bf16[96,4096]{1,0:T(8,128)(2,1)S(1)} %get-tuple-element.29), channel_id=1, source_target_pairs={{0,2},{1,3},{2,0},{3,1},{4,6},{5,7},{6,4},{7,5},{8,10},{9,11},{10,... | collective-permute-start | bytes 2359304 | tf_op jit(solution)/shard_map/ppermute | solution.py:167
  166.7 24.0 %collective-permute-start.16 = (bf16[96,4096]{1,0:T(8,128)(2,1)S(1)}, bf16[96,4096]{1,0:T(8,128)(2,1)S(1)}, u32[]{:S(2)}, u32[]{:S(2)}) collective-permute-start(bf16[96,4096]{1,0:T(8,128)(2,1)S(1)} %slice_select_fusion), channel_id=1, source_target_pairs={{0,4},{1,5},{2,6},{3,7},{4,8},{5,9},{6,10},{7,11},{8,12},{9,13},{1... | collective-permute-start | bytes 2359304 | tf_op jit(solution)/shard_map/ppermute | solution.py:176
  168.7 18.4 %collective-permute-start.17 = (bf16[96,4096]{1,0:T(8,128)(2,1)S(1)}, bf16[96,4096]{1,0:T(8,128)(2,1)S(1)}, u32[]{:S(2)}, u32[]{:S(2)}) collective-permute-start(bf16[96,4096]{1,0:T(8,128)(2,1)S(1)} %get-tuple-element.27), channel_id=1, source_target_pairs={{0,2},{1,3},{2,0},{3,1},{4,6},{5,7},{6,4},{7,5},{8,10},{9,11},{10,... | collective-permute-start | bytes 2359304 | tf_op jit(solution)/shard_map/ppermute | solution.py:167
  198.5 2.8 %collective-permute-start.20 = (bf16[480,1024]{1,0:T(8,128)(2,1)S(1)}, bf16[480,1024]{1,0:T(8,128)(2,1)}, u32[]{:S(2)}, u32[]{:S(2)}) collective-permute-start(bf16[480,1024]{1,0:T(8,128)(2,1)S(1)} %shard_map.63), channel_id=1, source_target_pairs={{0,16},{16,0},{1,17},{17,1},{2,18},{18,2},{3,19},{19,3},{4,20},{20... | collective-permute-start | bytes 2949128 | tf_op jit(solution)/shard_map/ppermute | solution.py:182
  205.2 16.3 %collective-permute-start.21 = (bf16[2,4,96,768]{3,2,1,0:T(8,128)(2,1)S(1)}, bf16[2,4,96,768]{3,2,1,0:T(8,128)(2,1)S(1)}, u32[]{:S(2)}, u32[]{:S(2)}) collective-permute-start(bf16[2,4,96,768]{3,2,1,0:T(8,128)(2,1)S(1)} %bitcast.81), channel_id=1, source_target_pairs={{0,1},{1,0},{2,3},{3,2},{4,5},{5,4},{6,7},{7,6},{8,9},{9,8},{10,11... | collective-permute-start | bytes 3538952 | tf_op jit(solution)/shard_map/ppermute | solution.py:234
  221.8 14.5 %copy-start.3 = (f32[768]{0:T(1024)S(1)}, f32[768]{0:T(1024)}, u32[]{:S(2)}) copy-start(f32[768]{0:T(1024)} %param.7) | copy-start | bytes 9220
  221.8 14.5 %copy-start.4 = (f32[2]{0:T(128)S(1)}, f32[2]{0:T(128)}, u32[]{:S(2)}) copy-start(f32[2]{0:T(128)} %param.6) | copy-start | bytes 28
  221.8 9.9 %collective-permute-start.22 = (bf16[4,96,768]{2,1,0:T(8,128)(2,1)S(1)}, bf16[4,96,768]{2,1,0:T(8,128)(2,1)S(1)}, u32[]{:S(2)}, u32[]{:S(2)}) collective-permute-start(bf16[4,96,768]{2,1,0:T(8,128)(2,1)S(1)} %fusion.1), channel_id=1, source_target_pairs={{0,2},{1,3},{2,0},{3,1},{4,6},{5,7},{6,4},{7,5},{8,10},{9,11},{10,... | collective-permute-start | bytes 1769480 | tf_op jit(solution)/shard_map/ppermute | solution.py:236
  232.7 18.2 %all-to-all-start = ((bf16[4,96,768]{2,1,0:T(8,128)(2,1)}), bf16[4,96,768]{2,1,0:T(8,128)(2,1)S(1)}, u32[]{:S(2)}, u32[]{:S(2)}) async-start(bf16[4,96,768]{2,1,0:T(8,128)(2,1)} %get-tuple-element.34), calls=%async_computation | async-start | bytes 1179648 | tf_op jit(solution)/shard_map/all_to_all | solution.py:240

commit v3 on v2

--- a/solution.py
+++ b/solution.py
@@ -235,14 +235,18 @@
     kept = tiles_for([0, turn[1]]) + came.astype(jnp.float32)
     came = lax.ppermute(kept[1].astype(jnp.bfloat16), AXES, everywhere(TURN[::-1]))
     sums = kept[0] + came.astype(jnp.float32)
-    chips = [list(range(z * PLANE, (z + 1) * PLANE)) for z in range(LAYERS)]
-    columns = [list(group) for group in zip(*chips)]
-    tiles = lax.all_to_all(
-        sums.astype(jnp.bfloat16), "pair", 0, 0, tiled=True, axis_index_groups=columns
-    )
-    own_sum = lax.dynamic_index_in_dim(sums, layer, 0, keepdims=False)
-    is_own = (jnp.arange(LAYERS) == layer)[:, None, None]
-    tiles = jnp.where(is_own, own_sum[None], tiles.astype(jnp.float32))
+    terms = [lax.dynamic_index_in_dim(sums, layer, 0, keepdims=False)]
+    for way in range(1, LAYERS):
+        to = (layer + way) % LAYERS
+        piece = lax.dynamic_index_in_dim(sums, to, 0, keepdims=False).astype(jnp.bfloat16)
+        count = LAYERS * PLANE
+        pairs = [
+            (core * count + i, core * count + (i + way * PLANE) % count)
+            for core in range(2)
+            for i in range(count)
+        ]
+        terms.append(lax.ppermute(piece, AXES, pairs).astype(jnp.float32))
+    tiles = jnp.stack(terms)
     return outputs(tiles, occ_energy, virt_energy)
 
 

time: 267 us -> 264 us (0.989)
  waiting for transfers between devices: 117 us -> 112 us
    all_to_all x1 -> x0, waiting for transfers between devices: 14.4 us -> none  [shards_stacked(): lax.all_to_all(sums.astype(jnp.bfloat16), 'pair', 0, 0, tiled=True, axis_...]
    ppermute x0 -> x3, waiting for transfers between devices: none -> 10.1 us  [shards_stacked(): terms.append(lax.ppermute(piece, AXES, pairs).astype(jnp.float32))]
    ppermute x0 -> x3, starting transfers between devices: none -> 3.87 us  [shards_stacked(): terms.append(lax.ppermute(piece, AXES, pairs).astype(jnp.float32))]
    all_to_all x1 -> x0, starting transfers between devices: 3.48 us -> none  [shards_stacked(): lax.all_to_all(sums.astype(jnp.bfloat16), 'pair', 0, 0, tiled=True, axis_...]
  transfers between devices with their start and end apart: 24 -> 26, of which waited for: 13 -> 14; matrix products, arithmetic and copies ran while one was open for 2% -> 2% of each run, Pallas kernels for 15% -> 15%
where the time goes in v3:
time: 264 us; the launch traced here: 263 us
  waiting for transfers between devices  112 us (42%)
  starting transfers between devices  74.5 us (28%)
  Pallas kernels  47.9 us (18%)
  blocking collectives  11.1 us (4%)
  other arithmetic  8.36 us (3%)
  between operations  3.23 us (1%)
  matrix products  2.87 us (1%)
  local copies, waits for them, and re-layouts  2.7 us (1%)
    ppermute x5, waiting for transfers between devices, climb(): return lax.ppermute(tied(piece, after), AXES, climbs(stage))  62.1 us
    pallas_call x5, Pallas kernels, fit(): pl.pallas_call(functools.partial(fit_kernel, len(pieces)), out_shape=jax....  47.9 us
    ppermute x12, starting transfers between devices, cross(): crossed.append(lax.ppermute(tied(piece, after), AXES, along(turn)))  36.4 us
    ppermute x5, starting transfers between devices, climb(): return lax.ppermute(tied(piece, after), AXES, climbs(stage))  31.4 us
    ppermute x12, waiting for transfers between devices, cross(): crossed.append(lax.ppermute(tied(piece, after), AXES, along(turn)))  15.2 us
    ppermute x1, waiting for transfers between devices, shards_stacked(): came = lax.ppermute(sent, AXES, everywhere(TURN))  14.1 us
    all_to_all x1, blocking collectives, total_of(): return jnp.sum(lax.all_to_all(sent, axes, 0, 0, tiled=True)[:, 0, 0])  11.1 us
    ppermute x3, waiting for transfers between devices, shards_stacked(): terms.append(lax.ppermute(piece, AXES, pairs).astype(jnp.float32))  10.1 us
  transfers between devices with their start and end apart: 26, of which 14 were waited for; matrix products, arithmetic and copies ran while one was open for 2% of the time, Pallas kernels for 15%

profile of v3, /device:TPU:0, one launch (start us, length us, event | category | flops | bytes accessed | tf_op | source)
XLA Modules:
  0.0 263.0 jit_solution(11717351612447439291)
XLA Ops:
  0.6 4.9 %collective-permute-start.4 = (bf16[96,8192]{1,0:T(8,128)(2,1)}, bf16[96,8192]{1,0:T(8,128)(2,1)}, u32[]{:S(2)}, u32[]{:S(2)}) collective-permute-start(bf16[96,8192]{1,0:T(8,128)(2,1)} %bitcast.82), channel_id=1, source_target_pairs={{0,4},{1,5},{2,6},{3,7},{4,8},{5,9},{6,10},{7,11},{8,12},{9,13},{1... | collective-permute-start | bytes 4718600 | tf_op jit(solution)/shard_map/ppermute | solution.py:176
  5.6 3.4 %collective-permute-start.1 = (bf16[96,8192]{1,0:T(8,128)(2,1)}, bf16[96,8192]{1,0:T(8,128)(2,1)S(1)}, u32[]{:S(2)}, u32[]{:S(2)}) collective-permute-start(bf16[96,8192]{1,0:T(8,128)(2,1)} %bitcast.83), channel_id=1, source_target_pairs={{0,2},{1,3},{2,0},{3,1},{4,6},{5,7},{6,4},{7,5},{8,10},{9,11},{10,... | collective-permute-start | bytes 4718600 | tf_op jit(solution)/shard_map/ppermute | solution.py:167
  9.0 3.4 %collective-permute-start = (bf16[96,8192]{1,0:T(8,128)(2,1)}, bf16[96,8192]{1,0:T(8,128)(2,1)S(1)}, u32[]{:S(2)}, u32[]{:S(2)}) collective-permute-start(bf16[96,8192]{1,0:T(8,128)(2,1)} %bitcast.84), channel_id=1, source_target_pairs={{0,1},{1,0},{2,3},{3,2},{4,5},{5,4},{6,7},{7,6},{8,9},{9,8},{10,11... | collective-permute-start | bytes 4718600 | tf_op jit(solution)/shard_map/ppermute | solution.py:167
  12.4 27.1 %collective-permute-done.4.refs_0_ = bf16[96,8192]{1,0:T(8,128)(2,1)} collective-permute-done((bf16[96,8192]{1,0:T(8,128)(2,1)}, bf16[96,8192]{1,0:T(8,128)(2,1)}, u32[]{:S(2)}, u32[]{:S(2)}) %collective-permute-start.4) | collective-permute-done | bytes 1572896 | tf_op jit(solution)/shard_map/ppermute | solution.py:176
  39.5 3.4 %collective-permute-start.5 = (bf16[96,8192]{1,0:T(8,128)(2,1)}, bf16[96,8192]{1,0:T(8,128)(2,1)}, u32[]{:S(2)}, u32[]{:S(2)}) collective-permute-start(bf16[96,8192]{1,0:T(8,128)(2,1)} %collective-permute-done.4.refs_0_), channel_id=1, source_target_pairs={{0,1},{1,0},{2,3},{3,2},{4,5},{5,4},{6,7},{7,6},{8,9},{9,8},{10,11... | collective-permute-start | bytes 4718600 | tf_op jit(solution)/shard_map/ppermute | solution.py:167
  44.1 4.4 %collective-permute-start.9 = (bf16[96,8192]{1,0:T(8,128)(2,1)}, bf16[96,8192]{1,0:T(8,128)(2,1)S(1)}, u32[]{:S(2)}, u32[]{:S(2)}) collective-permute-start(bf16[96,8192]{1,0:T(8,128)(2,1)} %collective-permute-done.4.refs_0_), channel_id=1, source_target_pairs={{0,4},{1,5},{2,6},{3,7},{4,8},{5,9},{6,10},{7,11},{8,12},{9,13},{1... | collective-permute-start | bytes 4718600 | tf_op jit(solution)/shard_map/ppermute | solution.py:176
  48.5 3.4 %collective-permute-start.2 = (bf16[96,8192]{1,0:T(8,128)(2,1)S(1)}, bf16[96,8192]{1,0:T(8,128)(2,1)}, u32[]{:S(2)}, u32[]{:S(2)}) collective-permute-start(bf16[96,8192]{1,0:T(8,128)(2,1)S(1)} %collective-permute-done.refs_1_), channel_id=1, source_target_pairs={{0,2},{1,3},{2,0},{3,1},{4,6},{5,7},{6,4},{7,5},{8,10},{9,11},{10,... | collective-permute-start | bytes 4718600 | tf_op jit(solution)/shard_map/ppermute | solution.py:167
  52.0 2.7 %collective-permute-start.6 = (bf16[96,8192]{1,0:T(8,128)(2,1)}, bf16[96,8192]{1,0:T(8,128)(2,1)S(1)}, u32[]{:S(2)}, u32[]{:S(2)}) collective-permute-start(bf16[96,8192]{1,0:T(8,128)(2,1)} %collective-permute-done.4.refs_0_), channel_id=1, source_target_pairs={{0,2},{1,3},{2,0},{3,1},{4,6},{5,7},{6,4},{7,5},{8,10},{9,11},{10,... | collective-permute-start | bytes 4718600 | tf_op jit(solution)/shard_map/ppermute | solution.py:167
  54.7 7.4 %collective-permute-done.5.refs_1_ = bf16[96,8192]{1,0:T(8,128)(2,1)} collective-permute-done((bf16[96,8192]{1,0:T(8,128)(2,1)}, bf16[96,8192]{1,0:T(8,128)(2,1)}, u32[]{:S(2)}, u32[]{:S(2)}) %collective-permute-start.5) | collective-permute-done | bytes 1572896 | tf_op jit(solution)/shard_map/ppermute | solution.py:167
  62.1 3.4 %collective-permute-start.7 = (bf16[96,8192]{1,0:T(8,128)(2,1)}, bf16[96,8192]{1,0:T(8,128)(2,1)S(1)}, u32[]{:S(2)}, u32[]{:S(2)}) collective-permute-start(bf16[96,8192]{1,0:T(8,128)(2,1)} %collective-permute-done.5.refs_1_), channel_id=1, source_target_pairs={{0,2},{1,3},{2,0},{3,1},{4,6},{5,7},{6,4},{7,5},{8,10},{9,11},{10,... | collective-permute-start | bytes 4718600 | tf_op jit(solution)/shard_map/ppermute | solution.py:167
  65.6 3.5 %collective-permute-done.9.refs_0_ = bf16[96,8192]{1,0:T(8,128)(2,1)S(1)} collective-permute-done((bf16[96,8192]{1,0:T(8,128)(2,1)}, bf16[96,8192]{1,0:T(8,128)(2,1)S(1)}, u32[]{:S(2)}, u32[]{:S(2)}) %collective-permute-start.9) | collective-permute-done | bytes 1572896 | tf_op jit(solution)/shard_map/ppermute | solution.py:176
  70.9 2.4 collective-permute-start.10
  74.9 15.9 %collective-permute-start.14 = (bf16[96,8192]{1,0:T(8,128)(2,1)S(1)}, bf16[96,8192]{1,0:T(8,128)(2,1)S(1)}, u32[]{:S(2)}, u32[]{:S(2)}) collective-permute-start(bf16[96,8192]{1,0:T(8,128)(2,1)S(1)} %broadcast_select_fusion.1), channel_id=1, source_target_pairs={{0,4},{1,5},{2,6},{3,7},{4,8},{5,9},{6,10},{7,11},{8,12},{9,13},{1... | collective-permute-start | bytes 4718600 | tf_op jit(solution)/shard_map/ppermute | solution.py:176
  90.8 3.4 %collective-permute-start.11 = (bf16[96,8192]{1,0:T(8,128)(2,1)S(1)}, bf16[96,8192]{1,0:T(8,128)(2,1)S(1)}, u32[]{:S(2)}, u32[]{:S(2)}) collective-permute-start(bf16[96,8192]{1,0:T(8,128)(2,1)S(1)} %collective-permute-done.9.refs_0_), channel_id=1, source_target_pairs={{0,2},{1,3},{2,0},{3,1},{4,6},{5,7},{6,4},{7,5},{8,10},{9,11},{10,... | collective-permute-start | bytes 4718600 | tf_op jit(solution)/shard_map/ppermute | solution.py:167
  94.3 11.1 %shard_map.59 = bf16[384,1024]{1,0:T(8,128)(2,1)S(1)} custom-call(s32[2]{0:T(128)S(1)} %add_convert_fusion.4.flags, bf16[96,8192]{1,0:T(8,128)(2,1)S(1)} %bitcast.85, bf16[96,8192]{1,0:T(8,128)(2,1)S(1)} %collective-permute-done.refs_1_, bf16[96,8192]{1,0:T(8,128)(2,1)S(1)} %copy-done.2, bf16[96,8192]{1,0:T(8,128)(2,1)} %collective-permute-done.2.refs_3_, ...), custom_call_target="tpu_custom_call" | custom-call | flops 6442450944 | bytes 23855104 | tf_op jit(solution)/shard_map/pallas_call | solution.py:131
  108.2 4.3 %collective-permute-start.15 = (bf16[96,8192]{1,0:T(8,128)(2,1)S(1)}, bf16[96,8192]{1,0:T(8,128)(2,1)S(1)}, u32[]{:S(2)}, u32[]{:S(2)}) collective-permute-start(bf16[96,8192]{1,0:T(8,128)(2,1)S(1)} %broadcast_select_fusion), channel_id=1, source_target_pairs={{0,4},{1,5},{2,6},{3,7},{4,8},{5,9},{6,10},{7,11},{8,12},{9,13},{1... | collective-permute-start | bytes 4718600 | tf_op jit(solution)/shard_map/ppermute | solution.py:176
  112.8 11.7 %shard_map.60 = bf16[384,1024]{1,0:T(8,128)(2,1)S(1)} custom-call(s32[2]{0:T(128)S(1)} %add_convert_fusion.4.flags, bf16[96,8192]{1,0:T(8,128)(2,1)} %collective-permute-done.4.refs_0_, bf16[96,8192]{1,0:T(8,128)(2,1)} %collective-permute-done.5.refs_1_, bf16[96,8192]{1,0:T(8,128)(2,1)S(1)} %collective-permute-done.6.refs_2_, ...), custom_call_target="tpu_custom_call" | custom-call | flops 6442450944 | bytes 23855104 | tf_op jit(solution)/shard_map/pallas_call | solution.py:131
  124.5 2.5 collective-permute-done.14.refs_1_
  127.1 2.4 collective-permute-start.18
  129.5 9.7 %shard_map.61 = bf16[288,1024]{1,0:T(8,128)(2,1)S(1)} custom-call(s32[2]{0:T(128)S(1)} %add_convert_fusion.4.flags, bf16[96,8192]{1,0:T(8,128)(2,1)S(1)} %collective-permute-done.9.refs_0_, bf16[96,8192]{1,0:T(8,128)(2,1)S(1)} %collective-permute-done.10.refs_1_, bf16[96,8192]{1,0:T(8,128)(2,1)S(1)} %collective-permute-done.11.refs_2_, ...), custom_call_target="tpu_custom_call" | custom-call | flops 4831838208 | bytes 22085632 | tf_op jit(solution)/shard_map/pallas_call | solution.py:131
  139.3 25.3 %collective-permute-done.15.refs_2_ = bf16[96,8192]{1,0:T(8,128)(2,1)S(1)} collective-permute-done((bf16[96,8192]{1,0:T(8,128)(2,1)S(1)}, bf16[96,8192]{1,0:T(8,128)(2,1)S(1)}, u32[]{:S(2)}, u32[]{:S(2)}) %collective-permute-start.15) | collective-permute-done | bytes 1572896 | tf_op jit(solution)/shard_map/ppermute | solution.py:176
  168.7 4.1 %collective-permute-start.17 = (bf16[96,4096]{1,0:T(8,128)(2,1)S(1)}, bf16[96,4096]{1,0:T(8,128)(2,1)S(1)}, u32[]{:S(2)}, u32[]{:S(2)}) collective-permute-start(bf16[96,4096]{1,0:T(8,128)(2,1)S(1)} %get-tuple-element.27), channel_id=1, source_target_pairs={{0,2},{1,3},{2,0},{3,1},{4,6},{5,7},{6,4},{7,5},{8,10},{9,11},{10,... | collective-permute-start | bytes 2359304 | tf_op jit(solution)/shard_map/ppermute | solution.py:167
  173.3 5.3 %collective-permute-done.19.refs_4_ = bf16[96,4096]{1,0:T(8,128)(2,1)S(1)} collective-permute-done((bf16[96,4096]{1,0:T(8,128)(2,1)S(1)}, bf16[96,4096]{1,0:T(8,128)(2,1)S(1)}, u32[]{:S(2)}, u32[]{:S(2)}) %collective-permute-start.19) | collective-permute-done | bytes 786464 | tf_op jit(solution)/shard_map/ppermute | solution.py:167
  178.6 7.7 %shard_map.62.refs_6_ = f32[480,1024]{1,0:T(8,128)S(1)} custom-call(s32[2]{0:T(128)S(1)} %add_convert_fusion.4.flags, bf16[96,8192]{1,0:T(8,128)(2,1)S(1)} %collective-permute-done.13.refs_0_, bf16[96,8192]{1,0:T(8,128)(2,1)S(1)} %collective-permute-done.14.refs_1_, bf16[96,8192]{1,0:T(8,128)(2,1)S(1)} %collective-permute-done.15.refs_2_, ...), custom_call_target="tpu_custom_call" | custom-call | flops 4026531840 | bytes 13303808 | tf_op jit(solution)/shard_map/pallas_call | solution.py:131
  187.0 3.8 %collective-permute-done.16.refs_3_ = bf16[96,4096]{1,0:T(8,128)(2,1)S(1)} collective-permute-done((bf16[96,4096]{1,0:T(8,128)(2,1)S(1)}, bf16[96,4096]{1,0:T(8,128)(2,1)S(1)}, u32[]{:S(2)}, u32[]{:S(2)}) %collective-permute-start.16) | collective-permute-done | bytes 786464 | tf_op jit(solution)/shard_map/ppermute | solution.py:176
  190.8 7.7 %shard_map.63 = bf16[480,1024]{1,0:T(8,128)(2,1)S(1)} custom-call(s32[2]{0:T(128)S(1)} %add_convert_fusion.4.flags, bf16[96,8192]{1,0:T(8,128)(2,1)S(1)} %collective-permute-done.13.refs_0_, bf16[96,8192]{1,0:T(8,128)(2,1)S(1)} %collective-permute-done.14.refs_1_, bf16[96,8192]{1,0:T(8,128)(2,1)S(1)} %collective-permute-done.15.refs_2_, ...), custom_call_target="tpu_custom_call" | custom-call | flops 4026531840 | bytes 13303808 | tf_op jit(solution)/shard_map/pallas_call | solution.py:131
  207.4 14.1 %collective-permute-done.21 = bf16[2,4,96,768]{3,2,1,0:T(8,128)(2,1)S(1)} collective-permute-done((bf16[2,4,96,768]{3,2,1,0:T(8,128)(2,1)S(1)}, bf16[2,4,96,768]{3,2,1,0:T(8,128)(2,1)S(1)}, u32[]{:S(2)}, u32[]{:S(2)}) %collective-permute-start.21) | collective-permute-done | bytes 1179680 | tf_op jit(solution)/shard_map/ppermute | solution.py:234
  223.5 8.3 %collective-permute-done.22 = bf16[4,96,768]{2,1,0:T(8,128)(2,1)} collective-permute-done((bf16[4,96,768]{2,1,0:T(8,128)(2,1)S(1)}, bf16[4,96,768]{2,1,0:T(8,128)(2,1)}, u32[]{:S(2)}, u32[]{:S(2)}) %collective-permute-start.22) | collective-permute-done | bytes 589856 | tf_op jit(solution)/shard_map/ppermute | solution.py:236
  233.2 3.8 %collective-permute-start.25 = (bf16[96,768]{1,0:T(8,128)(2,1)S(1)}, bf16[96,768]{1,0:T(8,128)(2,1)S(1)}, u32[]{:S(2)}, u32[]{:S(2)}) collective-permute-start(bf16[96,768]{1,0:T(8,128)(2,1)S(1)} %get-tuple-element.61), channel_id=1, source_target_pairs={{0,12},{1,13},{2,14},{3,15},{4,0},{5,1},{6,2},{7,3},{8,4},{9,5},{1... | collective-permute-start | bytes 442376 | tf_op jit(solution)/shard_map/ppermute | solution.py:248
  237.2 4.6 %collective-permute-done.23 = bf16[96,768]{1,0:T(8,128)(2,1)S(1)} collective-permute-done((bf16[96,768]{1,0:T(8,128)(2,1)S(1)}, bf16[96,768]{1,0:T(8,128)(2,1)S(1)}, u32[]{:S(2)}, u32[]{:S(2)}) %collective-permute-start.23) | collective-permute-done | bytes 147488 | tf_op jit(solution)/shard_map/ppermute | solution.py:248
  241.9 5.5 %collective-permute-done.24 = bf16[96,768]{1,0:T(8,128)(2,1)S(1)} collective-permute-done((bf16[96,768]{1,0:T(8,128)(2,1)S(1)}, bf16[96,768]{1,0:T(8,128)(2,1)S(1)}, u32[]{:S(2)}, u32[]{:S(2)}) %collective-permute-start.24) | collective-permute-done | bytes 147488 | tf_op jit(solution)/shard_map/ppermute | solution.py:248
  249.5 11.1 %all_to_all.5 = f32[32,1,128]{2,1,0:T(1,128)S(1)} all-to-all(f32[32,1,128]{2,1,0:T(1,128)S(1)} %broadcast_in_dim.2), channel_id=1, replica_groups=mesh['aux'=2,'pair'=16] {'aux','pair'}, dimensions={0} | all-to-all | bytes 32768 | tf_op jit(solution)/shard_map/all_to_all | solution.py:19
  (68 shorter events, 27.9 us)
Async XLA Ops:
  0.6 38.9 %collective-permute-start.4 = (bf16[96,8192]{1,0:T(8,128)(2,1)}, bf16[96,8192]{1,0:T(8,128)(2,1)}, u32[]{:S(2)}, u32[]{:S(2)}) collective-permute-start(bf16[96,8192]{1,0:T(8,128)(2,1)} %bitcast.82), channel_id=1, source_target_pairs={{0,4},{1,5},{2,6},{3,7},{4,8},{5,9},{6,10},{7,11},{8,12},{9,13},{1... | collective-permute-start | bytes 4718600 | tf_op jit(solution)/shard_map/ppermute | solution.py:176
  5.6 37.3 %collective-permute-start.1 = (bf16[96,8192]{1,0:T(8,128)(2,1)}, bf16[96,8192]{1,0:T(8,128)(2,1)S(1)}, u32[]{:S(2)}, u32[]{:S(2)}) collective-permute-start(bf16[96,8192]{1,0:T(8,128)(2,1)} %bitcast.83), channel_id=1, source_target_pairs={{0,2},{1,3},{2,0},{3,1},{4,6},{5,7},{6,4},{7,5},{8,10},{9,11},{10,... | collective-permute-start | bytes 4718600 | tf_op jit(solution)/shard_map/ppermute | solution.py:167
  9.0 35.1 %collective-permute-start = (bf16[96,8192]{1,0:T(8,128)(2,1)}, bf16[96,8192]{1,0:T(8,128)(2,1)S(1)}, u32[]{:S(2)}, u32[]{:S(2)}) collective-permute-start(bf16[96,8192]{1,0:T(8,128)(2,1)} %bitcast.84), channel_id=1, source_target_pairs={{0,1},{1,0},{2,3},{3,2},{4,5},{5,4},{6,7},{7,6},{8,9},{9,8},{10,11... | collective-permute-start | bytes 4718600 | tf_op jit(solution)/shard_map/ppermute | solution.py:167
  39.5 22.6 %collective-permute-start.5 = (bf16[96,8192]{1,0:T(8,128)(2,1)}, bf16[96,8192]{1,0:T(8,128)(2,1)}, u32[]{:S(2)}, u32[]{:S(2)}) collective-permute-start(bf16[96,8192]{1,0:T(8,128)(2,1)} %collective-permute-done.4.refs_0_), channel_id=1, source_target_pairs={{0,1},{1,0},{2,3},{3,2},{4,5},{5,4},{6,7},{7,6},{8,9},{9,8},{10,11... | collective-permute-start | bytes 4718600 | tf_op jit(solution)/shard_map/ppermute | solution.py:167
  42.9 1.2 copy-start.1
  44.1 25.0 %collective-permute-start.9 = (bf16[96,8192]{1,0:T(8,128)(2,1)}, bf16[96,8192]{1,0:T(8,128)(2,1)S(1)}, u32[]{:S(2)}, u32[]{:S(2)}) collective-permute-start(bf16[96,8192]{1,0:T(8,128)(2,1)} %collective-permute-done.4.refs_0_), channel_id=1, source_target_pairs={{0,4},{1,5},{2,6},{3,7},{4,8},{5,9},{6,10},{7,11},{8,12},{9,13},{1... | collective-permute-start | bytes 4718600 | tf_op jit(solution)/shard_map/ppermute | solution.py:176
  48.5 22.4 %collective-permute-start.2 = (bf16[96,8192]{1,0:T(8,128)(2,1)S(1)}, bf16[96,8192]{1,0:T(8,128)(2,1)}, u32[]{:S(2)}, u32[]{:S(2)}) collective-permute-start(bf16[96,8192]{1,0:T(8,128)(2,1)S(1)} %collective-permute-done.refs_1_), channel_id=1, source_target_pairs={{0,2},{1,3},{2,0},{3,1},{4,6},{5,7},{6,4},{7,5},{8,10},{9,11},{10,... | collective-permute-start | bytes 4718600 | tf_op jit(solution)/shard_map/ppermute | solution.py:167
  52.0 42.3 %copy-start = (bf16[8192,96]{0,1:T(8,128)(2,1)S(1)}, bf16[8192,96]{0,1:T(8,128)(2,1)}, u32[]{:S(2)}) copy-start(bf16[8192,96]{0,1:T(8,128)(2,1)} %param.5) | copy-start | bytes 4718596
  52.0 42.3 %copy-start.2 = (bf16[96,8192]{1,0:T(8,128)(2,1)S(1)}, bf16[96,8192]{1,0:T(8,128)(2,1)}, u32[]{:S(2)}) copy-start(bf16[96,8192]{1,0:T(8,128)(2,1)} %copy-done.1) | copy-start | bytes 4718596
  52.0 53.5 %collective-permute-start.6 = (bf16[96,8192]{1,0:T(8,128)(2,1)}, bf16[96,8192]{1,0:T(8,128)(2,1)S(1)}, u32[]{:S(2)}, u32[]{:S(2)}) collective-permute-start(bf16[96,8192]{1,0:T(8,128)(2,1)} %collective-permute-done.4.refs_0_), channel_id=1, source_target_pairs={{0,2},{1,3},{2,0},{3,1},{4,6},{5,7},{6,4},{7,5},{8,10},{9,11},{10,... | collective-permute-start | bytes 4718600 | tf_op jit(solution)/shard_map/ppermute | solution.py:167
  62.1 50.6 %collective-permute-start.7 = (bf16[96,8192]{1,0:T(8,128)(2,1)}, bf16[96,8192]{1,0:T(8,128)(2,1)S(1)}, u32[]{:S(2)}, u32[]{:S(2)}) collective-permute-start(bf16[96,8192]{1,0:T(8,128)(2,1)} %collective-permute-done.5.refs_1_), channel_id=1, source_target_pairs={{0,2},{1,3},{2,0},{3,1},{4,6},{5,7},{6,4},{7,5},{8,10},{9,11},{10,... | collective-permute-start | bytes 4718600 | tf_op jit(solution)/shard_map/ppermute | solution.py:167
  70.9 34.5 %collective-permute-start.10 = (bf16[96,8192]{1,0:T(8,128)(2,1)S(1)}, bf16[96,8192]{1,0:T(8,128)(2,1)S(1)}, u32[]{:S(2)}, u32[]{:S(2)}) collective-permute-start(bf16[96,8192]{1,0:T(8,128)(2,1)S(1)} %collective-permute-done.9.refs_0_), channel_id=1, source_target_pairs={{0,1},{1,0},{2,3},{3,2},{4,5},{5,4},{6,7},{7,6},{8,9},{9,8},{10,11... | collective-permute-start | bytes 4718600 | tf_op jit(solution)/shard_map/ppermute | solution.py:167
  74.9 52.1 %collective-permute-start.14 = (bf16[96,8192]{1,0:T(8,128)(2,1)S(1)}, bf16[96,8192]{1,0:T(8,128)(2,1)S(1)}, u32[]{:S(2)}, u32[]{:S(2)}) collective-permute-start(bf16[96,8192]{1,0:T(8,128)(2,1)S(1)} %broadcast_select_fusion.1), channel_id=1, source_target_pairs={{0,4},{1,5},{2,6},{3,7},{4,8},{5,9},{6,10},{7,11},{8,12},{9,13},{1... | collective-permute-start | bytes 4718600 | tf_op jit(solution)/shard_map/ppermute | solution.py:176
  90.8 38.7 %collective-permute-start.11 = (bf16[96,8192]{1,0:T(8,128)(2,1)S(1)}, bf16[96,8192]{1,0:T(8,128)(2,1)S(1)}, u32[]{:S(2)}, u32[]{:S(2)}) collective-permute-start(bf16[96,8192]{1,0:T(8,128)(2,1)S(1)} %collective-permute-done.9.refs_0_), channel_id=1, source_target_pairs={{0,2},{1,3},{2,0},{3,1},{4,6},{5,7},{6,4},{7,5},{8,10},{9,11},{10,... | collective-permute-start | bytes 4718600 | tf_op jit(solution)/shard_map/ppermute | solution.py:167
  105.4 2.7 %collective-permute-start.3 = (bf16[384,1024]{1,0:T(8,128)(2,1)S(1)}, bf16[384,1024]{1,0:T(8,128)(2,1)S(1)}, u32[]{:S(2)}, u32[]{:S(2)}) collective-permute-start(bf16[384,1024]{1,0:T(8,128)(2,1)S(1)} %shard_map.59), channel_id=1, source_target_pairs={{0,16},{16,0},{1,17},{17,1},{2,18},{18,2},{3,19},{19,3},{4,20},{20... | collective-permute-start | bytes 2359304 | tf_op jit(solution)/shard_map/ppermute | solution.py:182
  105.5 33.7 %collective-permute-start.13 = (bf16[96,8192]{1,0:T(8,128)(2,1)S(1)}, bf16[96,8192]{1,0:T(8,128)(2,1)S(1)}, u32[]{:S(2)}, u32[]{:S(2)}) collective-permute-start(bf16[96,8192]{1,0:T(8,128)(2,1)S(1)} %collective-permute-done.10.refs_1_), channel_id=1, source_target_pairs={{0,2},{1,3},{2,0},{3,1},{4,6},{5,7},{6,4},{7,5},{8,10},{9,11},{10,... | collective-permute-start | bytes 4718600 | tf_op jit(solution)/shard_map/ppermute | solution.py:167
  108.2 56.4 %collective-permute-start.15 = (bf16[96,8192]{1,0:T(8,128)(2,1)S(1)}, bf16[96,8192]{1,0:T(8,128)(2,1)S(1)}, u32[]{:S(2)}, u32[]{:S(2)}) collective-permute-start(bf16[96,8192]{1,0:T(8,128)(2,1)S(1)} %broadcast_select_fusion), channel_id=1, source_target_pairs={{0,4},{1,5},{2,6},{3,7},{4,8},{5,9},{6,10},{7,11},{8,12},{9,13},{1... | collective-permute-start | bytes 4718600 | tf_op jit(solution)/shard_map/ppermute | solution.py:176
  124.5 48.6 %collective-permute-start.8 = (bf16[384,1024]{1,0:T(8,128)(2,1)S(1)}, bf16[384,1024]{1,0:T(8,128)(2,1)S(1)}, u32[]{:S(2)}, u32[]{:S(2)}) collective-permute-start(bf16[384,1024]{1,0:T(8,128)(2,1)S(1)} %shard_map.60), channel_id=1, source_target_pairs={{0,16},{16,0},{1,17},{17,1},{2,18},{18,2},{3,19},{19,3},{4,20},{20... | collective-permute-start | bytes 2359304 | tf_op jit(solution)/shard_map/ppermute | solution.py:182
  127.1 51.5 %collective-permute-start.18 = (bf16[96,4096]{1,0:T(8,128)(2,1)S(1)}, bf16[96,4096]{1,0:T(8,128)(2,1)S(1)}, u32[]{:S(2)}, u32[]{:S(2)}) collective-permute-start(bf16[96,4096]{1,0:T(8,128)(2,1)S(1)} %slice.31), channel_id=1, source_target_pairs={{0,2},{1,3},{2,0},{3,1},{4,6},{5,7},{6,4},{7,5},{8,10},{9,11},{10,... | collective-permute-start | bytes 2359304 | tf_op jit(solution)/shard_map/ppermute | solution.py:167
  139.2 29.5 %collective-permute-start.12 = (bf16[288,1024]{1,0:T(8,128)(2,1)S(1)}, bf16[288,1024]{1,0:T(8,128)(2,1)S(1)}, u32[]{:S(2)}, u32[]{:S(2)}) collective-permute-start(bf16[288,1024]{1,0:T(8,128)(2,1)S(1)} %shard_map.61), channel_id=1, source_target_pairs={{0,16},{16,0},{1,17},{17,1},{2,18},{18,2},{3,19},{19,3},{4,20},{20... | collective-permute-start | bytes 1769480 | tf_op jit(solution)/shard_map/ppermute | solution.py:182
  164.7 13.9 %collective-permute-start.19 = (bf16[96,4096]{1,0:T(8,128)(2,1)S(1)}, bf16[96,4096]{1,0:T(8,128)(2,1)S(1)}, u32[]{:S(2)}, u32[]{:S(2)}) collective-permute-start(bf16[96,4096]{1,0:T(8,128)(2,1)S(1)} %get-tuple-element.29), channel_id=1, source_target_pairs={{0,2},{1,3},{2,0},{3,1},{4,6},{5,7},{6,4},{7,5},{8,10},{9,11},{10,... | collective-permute-start | bytes 2359304 | tf_op jit(solution)/shard_map/ppermute | solution.py:167
  166.7 24.0 %collective-permute-start.16 = (bf16[96,4096]{1,0:T(8,128)(2,1)S(1)}, bf16[96,4096]{1,0:T(8,128)(2,1)S(1)}, u32[]{:S(2)}, u32[]{:S(2)}) collective-permute-start(bf16[96,4096]{1,0:T(8,128)(2,1)S(1)} %slice_select_fusion), channel_id=1, source_target_pairs={{0,4},{1,5},{2,6},{3,7},{4,8},{5,9},{6,10},{7,11},{8,12},{9,13},{1... | collective-permute-start | bytes 2359304 | tf_op jit(solution)/shard_map/ppermute | solution.py:176
  168.7 18.4 %collective-permute-start.17 = (bf16[96,4096]{1,0:T(8,128)(2,1)S(1)}, bf16[96,4096]{1,0:T(8,128)(2,1)S(1)}, u32[]{:S(2)}, u32[]{:S(2)}) collective-permute-start(bf16[96,4096]{1,0:T(8,128)(2,1)S(1)} %get-tuple-element.27), channel_id=1, source_target_pairs={{0,2},{1,3},{2,0},{3,1},{4,6},{5,7},{6,4},{7,5},{8,10},{9,11},{10,... | collective-permute-start | bytes 2359304 | tf_op jit(solution)/shard_map/ppermute | solution.py:167
  198.5 2.8 %collective-permute-start.20 = (bf16[480,1024]{1,0:T(8,128)(2,1)S(1)}, bf16[480,1024]{1,0:T(8,128)(2,1)}, u32[]{:S(2)}, u32[]{:S(2)}) collective-permute-start(bf16[480,1024]{1,0:T(8,128)(2,1)S(1)} %shard_map.63), channel_id=1, source_target_pairs={{0,16},{16,0},{1,17},{17,1},{2,18},{18,2},{3,19},{19,3},{4,20},{20... | collective-permute-start | bytes 2949128 | tf_op jit(solution)/shard_map/ppermute | solution.py:182
  205.2 16.3 %collective-permute-start.21 = (bf16[2,4,96,768]{3,2,1,0:T(8,128)(2,1)S(1)}, bf16[2,4,96,768]{3,2,1,0:T(8,128)(2,1)S(1)}, u32[]{:S(2)}, u32[]{:S(2)}) collective-permute-start(bf16[2,4,96,768]{3,2,1,0:T(8,128)(2,1)S(1)} %bitcast.95), channel_id=1, source_target_pairs={{0,1},{1,0},{2,3},{3,2},{4,5},{5,4},{6,7},{7,6},{8,9},{9,8},{10,11... | collective-permute-start | bytes 3538952 | tf_op jit(solution)/shard_map/ppermute | solution.py:234
  221.8 10.1 %collective-permute-start.22 = (bf16[4,96,768]{2,1,0:T(8,128)(2,1)S(1)}, bf16[4,96,768]{2,1,0:T(8,128)(2,1)}, u32[]{:S(2)}, u32[]{:S(2)}) collective-permute-start(bf16[4,96,768]{2,1,0:T(8,128)(2,1)S(1)} %fusion.1), channel_id=1, source_target_pairs={{0,2},{1,3},{2,0},{3,1},{4,6},{5,7},{6,4},{7,5},{8,10},{9,11},{10,... | collective-permute-start | bytes 1769480 | tf_op jit(solution)/shard_map/ppermute | solution.py:236
  223.5 13.5 %copy-start.3 = (f32[768]{0:T(1024)S(1)}, f32[768]{0:T(1024)}, u32[]{:S(2)}) copy-start(f32[768]{0:T(1024)} %param.7) | copy-start | bytes 9220
  223.5 13.5 %copy-start.4 = (f32[2]{0:T(128)S(1)}, f32[2]{0:T(128)}, u32[]{:S(2)}) copy-start(f32[2]{0:T(128)} %param.6) | copy-start | bytes 28
  233.1 8.7 %collective-permute-start.23 = (bf16[96,768]{1,0:T(8,128)(2,1)S(1)}, bf16[96,768]{1,0:T(8,128)(2,1)S(1)}, u32[]{:S(2)}, u32[]{:S(2)}) collective-permute-start(bf16[96,768]{1,0:T(8,128)(2,1)S(1)} %get-tuple-element.60), channel_id=1, source_target_pairs={{0,4},{1,5},{2,6},{3,7},{4,8},{5,9},{6,10},{7,11},{8,12},{9,13},{1... | collective-permute-start | bytes 442376 | tf_op jit(solution)/shard_map/ppermute | solution.py:248
  233.2 8.7 %collective-permute-start.25 = (bf16[96,768]{1,0:T(8,128)(2,1)S(1)}, bf16[96,768]{1,0:T(8,128)(2,1)S(1)}, u32[]{:S(2)}, u32[]{:S(2)}) collective-permute-start(bf16[96,768]{1,0:T(8,128)(2,1)S(1)} %get-tuple-element.61), channel_id=1, source_target_pairs={{0,12},{1,13},{2,14},{3,15},{4,0},{5,1},{6,2},{7,3},{8,4},{9,5},{1... | collective-permute-start | bytes 442376 | tf_op jit(solution)/shard_map/ppermute | solution.py:248
  237.0 10.4 %collective-permute-start.24 = (bf16[96,768]{1,0:T(8,128)(2,1)S(1)}, bf16[96,768]{1,0:T(8,128)(2,1)S(1)}, u32[]{:S(2)}, u32[]{:S(2)}) collective-permute-start(bf16[96,768]{1,0:T(8,128)(2,1)S(1)} %get-tuple-element.62), channel_id=1, source_target_pairs={{0,8},{1,9},{2,10},{3,11},{4,12},{5,13},{6,14},{7,15},{8,0},{9,1},... | collective-permute-start | bytes 442376 | tf_op jit(solution)/shard_map/ppermute | solution.py:248
